TPU v7x, 256 devices: a whole 4x4x8 slice. The times are simulated.
256 devices in a mesh: section: 16 (over z, x_lo), dp: 16 (over y, x_hi, core).
Axes of the slice: x: 4 (x_hi: 2, x_lo: 2; x = x_hi * 2 + x_lo), y: 4, z: 8, core: 2. Of those that a mesh axis runs over, the one named last changes fastest.
Arguments:
- coeffs: bfloat16 [2, 2048, 256], P(None, 'dp'), may hold values from -6 to 6
- cotangent: bfloat16 [2, 2048, 256], P(None, 'dp'), may hold values from -0.1875 to 0.1875
- segment_ids: int32 [2, 2048], P(None, 'dp'), may hold values from 0 to 127, never falling along the last dimension, each value on 1 to 32 neighbouring positions
- basis_matrix: bfloat16 [4096, 256], replicated, may hold values from -0.375 to 0.375
- section_gains: float32 [16, 4096], P('section'), may hold values from 0.5 to 1.5
- value_weight: bfloat16 [16, 4096, 1024], P('section'), may hold values from -0.09375 to 0.09375
- out_weight: bfloat16 [16, 1024, 256], P('section'), may hold values from -0.1875 to 0.1875
Outputs:
- grad_value: float32 [16, 4096, 1024], P('section', 'dp')
- grad_out: float32 [16, 1024, 256], P('section', 'dp')
- grad_gain: float32 [16, 4096], P('section', 'dp')
All inputs are finite; a program needn't handle non-finite values.
Results may differ from a plain program's by a relative error of at most 0.034.
Values may be sent and summed in bfloat16 or wider, within the bound.
A program may use at most 128 MiB of HBM per device.

v0:
```python
import jax
import jax.numpy as jnp
from jax import lax
from jax.sharding import PartitionSpec as P

EPS = 1e-05


def passed_along(value, axis, by):
    peers = lax.axis_size(axis)
    pairs = [(i, i + by) for i in range(peers) if 0 <= i + by < peers]
    return lax.ppermute(value, axis, pairs)


def mixing_table(segments):
    positions = jnp.arange(segments.shape[0])
    same_segment = (segments[:, None] == segments[None, :]) & (
        positions[:, None] >= positions[None, :]
    )
    weights = same_segment.astype(jnp.float32)
    return (weights / jnp.sum(weights, axis=1, keepdims=True)).astype(jnp.bfloat16)


def normalize(section_coeff, basis_matrix):
    rebuilt = jnp.dot(section_coeff, basis_matrix.T, preferred_element_type=jnp.float32)
    inv_rms = lax.rsqrt(jnp.mean(rebuilt * rebuilt, axis=1, keepdims=True) + EPS)
    return (rebuilt, inv_rms)


def section_forward(
    section_coeff, segments, basis_matrix, section_gain, section_value, section_out
):
    mixing = mixing_table(segments)
    rebuilt, inv_rms = normalize(section_coeff, basis_matrix)
    normed = (rebuilt * inv_rms * section_gain).astype(jnp.bfloat16)
    values = jnp.dot(normed, section_value, preferred_element_type=jnp.float32).astype(jnp.bfloat16)
    pooled = jnp.dot(mixing, values, preferred_element_type=jnp.float32).astype(jnp.bfloat16)
    update = jnp.dot(pooled, section_out, preferred_element_type=jnp.float32)
    return ((section_coeff.astype(jnp.float32) + update).astype(jnp.bfloat16), pooled)


def section_backward(
    grad_next,
    section_coeff,
    pooled,
    segments,
    basis_matrix,
    section_gain,
    section_value,
    section_out,
):
    mixing = mixing_table(segments)
    rebuilt, inv_rms = normalize(section_coeff, basis_matrix)
    grad_out = jnp.dot(pooled.T, grad_next, preferred_element_type=jnp.float32)
    back_pooled = jnp.dot(grad_next, section_out.T, preferred_element_type=jnp.float32).astype(
        jnp.bfloat16
    )
    back_values = jnp.dot(mixing.T, back_pooled, preferred_element_type=jnp.float32).astype(
        jnp.bfloat16
    )
    scaled_coeff = (section_coeff.astype(jnp.float32) * inv_rms).astype(jnp.bfloat16)
    factor = jnp.dot(scaled_coeff.T, back_values, preferred_element_type=jnp.float32)
    back_normed = jnp.dot(back_values, section_value.T, preferred_element_type=jnp.float32)
    unit_rows = rebuilt * inv_rms
    grad_gain = jnp.sum(back_normed * unit_rows, axis=0)
    back_unit = back_normed * section_gain
    back_rebuilt = (
        inv_rms * (back_unit - unit_rows * jnp.mean(back_unit * unit_rows, axis=1, keepdims=True))
    ).astype(jnp.bfloat16)
    grad_now = (
        grad_next.astype(jnp.float32)
        + jnp.dot(back_rebuilt, basis_matrix, preferred_element_type=jnp.float32)
    ).astype(jnp.bfloat16)
    return (grad_now, factor, grad_out, grad_gain)


def shards(coeffs, cotangent, segment_ids, basis_matrix, section_gains, value_weight, out_weight):
    sections = lax.axis_size("section")
    section_id = lax.axis_index("section")
    micro_count = coeffs.shape[0]
    row_count = coeffs.shape[1]
    sub_width = coeffs.shape[2]
    section_gain = section_gains[0]
    section_value = value_weight[0]
    section_out = out_weight[0]
    model_width = section_value.shape[0]
    inner_width = section_value.shape[1]
    turns = micro_count + sections - 1

    def forward_turn(turn_index, loop_state):
        incoming, saved_coeff, saved_pooled = loop_state
        micro_index = turn_index - section_id
        active = (micro_index >= 0) & (micro_index < micro_count)
        clipped = jnp.clip(micro_index, 0, micro_count - 1)
        own_coeff = lax.dynamic_index_in_dim(coeffs, clipped, 0, keepdims=False)
        section_coeff = jnp.where(section_id == 0, own_coeff, incoming)
        segments = lax.dynamic_index_in_dim(segment_ids, clipped, 0, keepdims=False)

        def run_section(operands):
            return section_forward(
                operands[0], operands[1], basis_matrix, section_gain, section_value, section_out
            )

        def skip_section(operands):
            return (
                jnp.zeros((row_count, sub_width), jnp.bfloat16),
                jnp.zeros((row_count, inner_width), jnp.bfloat16),
            )

        outgoing, pooled = lax.cond(active, run_section, skip_section, (section_coeff, segments))
        saved_coeff = jnp.where(
            active,
            lax.dynamic_update_index_in_dim(saved_coeff, section_coeff, clipped, 0),
            saved_coeff,
        )
        saved_pooled = jnp.where(
            active, lax.dynamic_update_index_in_dim(saved_pooled, pooled, clipped, 0), saved_pooled
        )
        incoming = passed_along(outgoing, "section", 1)
        return (incoming, saved_coeff, saved_pooled)

    initial = (
        jnp.zeros((row_count, sub_width), jnp.bfloat16),
        jnp.zeros((micro_count, row_count, sub_width), jnp.bfloat16),
        jnp.zeros((micro_count, row_count, inner_width), jnp.bfloat16),
    )
    ignored, saved_coeff, saved_pooled = lax.fori_loop(0, turns, forward_turn, initial)

    def backward_turn(turn_index, loop_state):
        incoming, factor_sum, out_sum, gain_sum = loop_state
        micro_index = turn_index - (sections - 1 - section_id)
        active = (micro_index >= 0) & (micro_index < micro_count)
        clipped = jnp.clip(micro_index, 0, micro_count - 1)
        section_coeff = lax.dynamic_index_in_dim(saved_coeff, clipped, 0, keepdims=False)
        pooled = lax.dynamic_index_in_dim(saved_pooled, clipped, 0, keepdims=False)
        segments = lax.dynamic_index_in_dim(segment_ids, clipped, 0, keepdims=False)
        own_grad = lax.dynamic_index_in_dim(cotangent, clipped, 0, keepdims=False)
        grad_next = jnp.where(section_id == sections - 1, own_grad, incoming)

        def run_back(operands):
            return section_backward(
                operands[0],
                operands[1],
                operands[2],
                operands[3],
                basis_matrix,
                section_gain,
                section_value,
                section_out,
            )

        def skip_back(operands):
            return (
                jnp.zeros((row_count, sub_width), jnp.bfloat16),
                jnp.zeros((sub_width, inner_width), jnp.float32),
                jnp.zeros((inner_width, sub_width), jnp.float32),
                jnp.zeros((model_width,), jnp.float32),
            )

        grad_now, factor, grad_out, grad_gain = lax.cond(
            active, run_back, skip_back, (grad_next, section_coeff, pooled, segments)
        )
        incoming = passed_along(grad_now, "section", -1)
        return (incoming, factor_sum + factor, out_sum + grad_out, gain_sum + grad_gain)

    initial_back = (
        jnp.zeros((row_count, sub_width), jnp.bfloat16),
        jnp.zeros((sub_width, inner_width), jnp.float32),
        jnp.zeros((inner_width, sub_width), jnp.float32),
        jnp.zeros((model_width,), jnp.float32),
    )
    ignored_grad, factor_sum, out_sum, gain_sum = lax.fori_loop(
        0, turns, backward_turn, initial_back
    )
    scaled_basis = section_gain[:, None] * basis_matrix.astype(jnp.float32)
    partial_grad = jnp.dot(scaled_basis, factor_sum, precision=lax.Precision.HIGHEST)
    value_grad, out_grad, gain_grad = (
        lax.psum_scatter(
            partial_grad.astype(jnp.bfloat16), "dp", scatter_dimension=0, tiled=True
        ).astype(jnp.float32),
        lax.psum_scatter(
            out_sum.astype(jnp.bfloat16), "dp", scatter_dimension=0, tiled=True
        ).astype(jnp.float32),
        lax.psum_scatter(
            gain_sum.astype(jnp.bfloat16), "dp", scatter_dimension=0, tiled=True
        ).astype(jnp.float32),
    )
    return (value_grad[None], out_grad[None], gain_grad[None])


def solution(mesh):
    placed = (
        P(None, "dp", None),
        P(None, "dp", None),
        P(None, "dp"),
        P(),
        P("section", None),
        P("section", None, None),
        P("section", None, None),
    )
    return jax.shard_map(
        shards,
        mesh=mesh,
        in_specs=placed,
        out_specs=(P("section", "dp", None), P("section", "dp", None), P("section", "dp")),
        check_vma=False,
    )
```

profile of v0, /device:TPU:1, one launch (start us, length us, event | category | flops | bytes accessed | tf_op | source)
XLA Modules:
  0.0 890.3 jit_solution(5487802976943314758)
XLA Ops:
  8.8 213.8 %while.40 = (s32[]{:T(128)}, bf16[128,256]{1,0:T(8,128)(2,1)S(1)}, bf16[2,128,256]{2,1,0:T(8,128)(2,1)}, bf16[2,128,1024]{2,1,0:T(8,128)(2,1)}, s32[]{:T(128)}, ...) while((s32[]{:T(128)}, bf16[128,256]{1,0:T(8,128)(2,1)S(1)}, ...), condition=%wide.region_5.6_spmd, body=%wide.region_0.5_spmd.sunk | while | flops 1446199296 | bytes 19487608 | solution.py:127
  10.3 10.2 %conditional.5 = (bf16[128,256]{1,0:T(8,128)(2,1)S(1)}, bf16[1,128,1024]{2,1,0:T(8,128)(2,1)}) conditional(s32[]{:T(128)} %convert_element_type.152, () %tuple.107, (bf16[128,256]{1,0:T(8,128)(2,1)S(1)}, s32[2,128]{1,0:T(2,128)}, s32[]{:T(128)}, bf16[4096,256]{1,0:T(8,128)(2,1)}, f32[1,4096]{1,0:T(1,128)}, /*index=5*/bf16[4096,1024]{1,0:T(8,128)(2,1)}, ...), branch_computations={%region_1.1_spmd, %region_2.4_spmd} | conditional | flops 1446002688 | bytes 18109516 | solution.py:110
  11.2 2.5 multiply_reduce_fusion
  13.7 5.6 convolution_convert_fusion
  25.2 10.2 %conditional.5 = (bf16[128,256]{1,0:T(8,128)(2,1)S(1)}, bf16[1,128,1024]{2,1,0:T(8,128)(2,1)}) conditional(s32[]{:T(128)} %convert_element_type.152, () %tuple.107, (bf16[128,256]{1,0:T(8,128)(2,1)S(1)}, s32[2,128]{1,0:T(2,128)}, s32[]{:T(128)}, bf16[4096,256]{1,0:T(8,128)(2,1)}, f32[1,4096]{1,0:T(1,128)}, /*index=5*/bf16[4096,1024]{1,0:T(8,128)(2,1)}, ...), branch_computations={%region_1.1_spmd, %region_2.4_spmd} | conditional | flops 1446002688 | bytes 18109516 | solution.py:110
  26.0 2.5 multiply_reduce_fusion
  28.6 5.6 convolution_convert_fusion
  35.4 3.2 collective-permute-start
  42.6 12.6 %collective-permute-start = (bf16[128,256]{1,0:T(8,128)(2,1)S(1)}, bf16[128,256]{1,0:T(8,128)(2,1)S(1)}, u32[]{:S(2)}, u32[]{:S(2)}) collective-permute-start(bf16[128,256]{1,0:T(8,128)(2,1)S(1)} %get-tuple-element.990), channel_id=1, source_target_pairs={{0,16},{16,32},{32,48},{48,64},{64,80},{80,96},{96,112},{112,128},... | collective-permute-start | bytes 196616 | tf_op jit(solution)/shard_map/while/body/eval_jaxpr/ppermute | solution.py:12
  59.3 3.3 collective-permute-start
  66.5 13.2 %collective-permute-start = (bf16[128,256]{1,0:T(8,128)(2,1)S(1)}, bf16[128,256]{1,0:T(8,128)(2,1)S(1)}, u32[]{:S(2)}, u32[]{:S(2)}) collective-permute-start(bf16[128,256]{1,0:T(8,128)(2,1)S(1)} %get-tuple-element.990), channel_id=1, source_target_pairs={{0,16},{16,32},{32,48},{48,64},{64,80},{80,96},{96,112},{112,128},... | collective-permute-start | bytes 196616 | tf_op jit(solution)/shard_map/while/body/eval_jaxpr/ppermute | solution.py:12
  83.7 4.2 collective-permute-start
  91.9 10.5 %collective-permute-start = (bf16[128,256]{1,0:T(8,128)(2,1)S(1)}, bf16[128,256]{1,0:T(8,128)(2,1)S(1)}, u32[]{:S(2)}, u32[]{:S(2)}) collective-permute-start(bf16[128,256]{1,0:T(8,128)(2,1)S(1)} %get-tuple-element.990), channel_id=1, source_target_pairs={{0,16},{16,32},{32,48},{48,64},{64,80},{80,96},{96,112},{112,128},... | collective-permute-start | bytes 196616 | tf_op jit(solution)/shard_map/while/body/eval_jaxpr/ppermute | solution.py:12
  106.4 4.2 collective-permute-start
  114.6 11.3 %collective-permute-start = (bf16[128,256]{1,0:T(8,128)(2,1)S(1)}, bf16[128,256]{1,0:T(8,128)(2,1)S(1)}, u32[]{:S(2)}, u32[]{:S(2)}) collective-permute-start(bf16[128,256]{1,0:T(8,128)(2,1)S(1)} %get-tuple-element.990), channel_id=1, source_target_pairs={{0,16},{16,32},{32,48},{48,64},{64,80},{80,96},{96,112},{112,128},... | collective-permute-start | bytes 196616 | tf_op jit(solution)/shard_map/while/body/eval_jaxpr/ppermute | solution.py:12
  130.0 4.2 collective-permute-start
  138.1 10.5 %collective-permute-start = (bf16[128,256]{1,0:T(8,128)(2,1)S(1)}, bf16[128,256]{1,0:T(8,128)(2,1)S(1)}, u32[]{:S(2)}, u32[]{:S(2)}) collective-permute-start(bf16[128,256]{1,0:T(8,128)(2,1)S(1)} %get-tuple-element.990), channel_id=1, source_target_pairs={{0,16},{16,32},{32,48},{48,64},{64,80},{80,96},{96,112},{112,128},... | collective-permute-start | bytes 196616 | tf_op jit(solution)/shard_map/while/body/eval_jaxpr/ppermute | solution.py:12
  152.6 4.2 collective-permute-start
  160.8 11.4 %collective-permute-start = (bf16[128,256]{1,0:T(8,128)(2,1)S(1)}, bf16[128,256]{1,0:T(8,128)(2,1)S(1)}, u32[]{:S(2)}, u32[]{:S(2)}) collective-permute-start(bf16[128,256]{1,0:T(8,128)(2,1)S(1)} %get-tuple-element.990), channel_id=1, source_target_pairs={{0,16},{16,32},{32,48},{48,64},{64,80},{80,96},{96,112},{112,128},... | collective-permute-start | bytes 196616 | tf_op jit(solution)/shard_map/while/body/eval_jaxpr/ppermute | solution.py:12
  176.2 4.2 collective-permute-start
  184.4 10.5 %collective-permute-start = (bf16[128,256]{1,0:T(8,128)(2,1)S(1)}, bf16[128,256]{1,0:T(8,128)(2,1)S(1)}, u32[]{:S(2)}, u32[]{:S(2)}) collective-permute-start(bf16[128,256]{1,0:T(8,128)(2,1)S(1)} %get-tuple-element.990), channel_id=1, source_target_pairs={{0,16},{16,32},{32,48},{48,64},{64,80},{80,96},{96,112},{112,128},... | collective-permute-start | bytes 196616 | tf_op jit(solution)/shard_map/while/body/eval_jaxpr/ppermute | solution.py:12
  198.9 4.2 collective-permute-start
  207.0 13.8 %collective-permute-start = (bf16[128,256]{1,0:T(8,128)(2,1)S(1)}, bf16[128,256]{1,0:T(8,128)(2,1)S(1)}, u32[]{:S(2)}, u32[]{:S(2)}) collective-permute-start(bf16[128,256]{1,0:T(8,128)(2,1)S(1)} %get-tuple-element.990), channel_id=1, source_target_pairs={{0,16},{16,32},{32,48},{48,64},{64,80},{80,96},{96,112},{112,128},... | collective-permute-start | bytes 196616 | tf_op jit(solution)/shard_map/while/body/eval_jaxpr/ppermute | solution.py:12
  222.6 443.4 %while.41 = (s32[]{:T(128)}, bf16[128,256]{1,0:T(8,128)(2,1)S(1)}, f32[256,1024]{1,0:T(8,128)}, f32[1024,256]{1,0:T(8,128)}, f32[4096]{0:T(1024)}, /*index=5*/s3...) while((s32[]{:T(128)}, bf16[128,256]{1,0:T(8,128)(2,1)S(1)}, ...), condition=%wide.region_13.14_spmd.clone, body=%wide.region_6.13_spmd.clone.sunk | while | flops 1854558208 | bytes 50963016 | solution.py:172
  222.6 2.5 conditional.6
  236.3 2.7 select_add_fusion.6
  240.5 5.7 collective-permute-done.1
  246.2 2.5 conditional.6
  250.1 2.7 select_add_fusion.6
  254.2 2.5 collective-permute-done.1
  260.6 2.7 select_add_fusion.6
  264.7 5.9 collective-permute-done.1
  274.5 2.7 select_add_fusion.6
  278.7 3.0 collective-permute-done.1
  281.7 2.5 conditional.6
  285.6 2.7 select_add_fusion.6
  289.8 4.5 collective-permute-done.1
  298.1 2.7 select_add_fusion.6
  304.0 2.5 conditional.6
  307.8 2.7 select_add_fusion.6
  312.0 6.6 collective-permute-done.1
  322.5 2.7 select_add_fusion.6
  332.4 2.7 select_add_fusion.6
  336.6 5.5 collective-permute-done.1
  342.1 2.5 conditional.6
  346.0 2.7 select_add_fusion.6
  350.2 2.7 collective-permute-done.1
  356.7 2.7 select_add_fusion.6
  360.9 7.0 collective-permute-done.1
  371.8 2.7 select_add_fusion.6
  381.2 2.7 select_add_fusion.6
  385.3 6.3 collective-permute-done.1
  395.5 2.7 select_add_fusion.6
  399.7 218.0 %collective-permute-done.1 = bf16[128,256]{1,0:T(8,128)(2,1)S(1)} collective-permute-done((bf16[128,256]{1,0:T(8,128)(2,1)}, bf16[128,256]{1,0:T(8,128)(2,1)S(1)}, u32[]{:S(2)}, u32[]{:S(2)}) %collective-permute-start.1) | collective-permute-done | bytes 65568 | tf_op jit(solution)/shard_map/while/body/eval_jaxpr/ppermute | solution.py:12
  617.7 17.1 %conditional.6 = (bf16[128,256]{1,0:T(8,128)(2,1)}, f32[256,1024]{1,0:T(8,128)}, f32[1024,256]{1,0:T(8,128)S(1)}, f32[4096]{0:T(1024)}) conditional(s32[]{:T(128)} %convert_element_type.153, () %tuple.110, (pred[]{:T(512)}, s32[]{:T(128)}, bf16[2,128,256]{2,1,0:T(8,128)(2,1)}, bf16[128,256]{1,0:T(8,128)(2,1)S(1)}, bf16[2,128,256]{2,1,0:T(8,128)(2,1)}, ...), branch_computations={%region_7.7_spmd, %region_8.12_spmd} | conditional | flops 1853501440 | bytes 35840132 | solution.py:160
  626.4 7.1 multiply_reduce_fusion.1
  636.2 2.7 select_add_fusion.6
  642.7 17.1 %conditional.6 = (bf16[128,256]{1,0:T(8,128)(2,1)}, f32[256,1024]{1,0:T(8,128)}, f32[1024,256]{1,0:T(8,128)S(1)}, f32[4096]{0:T(1024)}) conditional(s32[]{:T(128)} %convert_element_type.153, () %tuple.110, (pred[]{:T(512)}, s32[]{:T(128)}, bf16[2,128,256]{2,1,0:T(8,128)(2,1)}, bf16[128,256]{1,0:T(8,128)(2,1)S(1)}, bf16[2,128,256]{2,1,0:T(8,128)(2,1)}, ...), branch_computations={%region_7.7_spmd, %region_8.12_spmd} | conditional | flops 1853501440 | bytes 35840132 | solution.py:160
  651.4 7.1 multiply_reduce_fusion.1
  661.2 2.7 select_add_fusion.6
  668.4 16.7 %convolution_convert_fusion.4 = bf16[4096,1024]{1,0:T(8,128)(2,1)} fusion(f32[256,1024]{1,0:T(8,128)} %get-tuple-element.714, bf16[4096,256]{1,0:T(8,128)(2,1)S(1)} %copy-done.1, f32[4096]{0:T(1024)} %bitcast.60), kind=kOutput, calls=%fused_computation.63 | convolution fusion | flops 12891193344 | bytes 11550720 | tf_op jit(solution)/shard_map/dot_general | solution.py:176
  687.0 66.0 %all-reduce = bf16[4096]{0:T(1024)(128)(2,1)S(1)} all-reduce(bf16[4096]{0:T(1024)(128)(2,1)S(1)} %convert_element_type.108), channel_id=4, replica_groups=mesh['section'=16,'dp'=16] {'dp'}, use_global_device_ids=true, to_apply=%region_16.17.clone | all-reduce | flops 4096 | bytes 16384
  753.6 12.5 %reduce-scatter.5.cloned.1.call-done = bf16[64,256]{1,0:T(8,128)(2,1)} async-done(((bf16[1024,256]{1,0:T(8,128)(2,1)}), bf16[64,256]{1,0:T(8,128)(2,1)}) %reduce-scatter.5.cloned.1.call-update) | async-done | bytes 32784 | tf_op jit(solution)/shard_map/reduce_scatter | solution.py:181
  767.5 113.8 %reduce-scatter.3.cloned.1.call-done = bf16[256,1024]{1,0:T(8,128)(2,1)} async-done(((bf16[4096,1024]{1,0:T(8,128)(2,1)}), bf16[256,1024]{1,0:T(8,128)(2,1)}) %reduce-scatter.3.cloned.1.call-update) | async-done | bytes 524304 | tf_op jit(solution)/shard_map/reduce_scatter | solution.py:178
  (428 shorter events, 234.2 us)
Async XLA Ops:
  7.2 759.0 %reduce-scatter.5.cloned.1.call-start = ((), (), s32[]{:S(2)}) async-start(), calls=%async_computation.3 | async-start | bytes 557056 | tf_op jit(solution)/shard_map/reduce_scatter | solution.py:181
  13.7 5.6 copy-start.2
  20.5 3.1 collective-permute-start
  28.6 5.6 copy-start.2
  35.4 5.0 collective-permute-start
  42.6 14.4 %collective-permute-start = (bf16[128,256]{1,0:T(8,128)(2,1)S(1)}, bf16[128,256]{1,0:T(8,128)(2,1)S(1)}, u32[]{:S(2)}, u32[]{:S(2)}) collective-permute-start(bf16[128,256]{1,0:T(8,128)(2,1)S(1)} %get-tuple-element.990), channel_id=1, source_target_pairs={{0,16},{16,32},{32,48},{48,64},{64,80},{80,96},{96,112},{112,128},... | collective-permute-start | bytes 196616 | tf_op jit(solution)/shard_map/while/body/eval_jaxpr/ppermute | solution.py:12
  59.3 5.0 collective-permute-start
  66.5 14.9 %collective-permute-start = (bf16[128,256]{1,0:T(8,128)(2,1)S(1)}, bf16[128,256]{1,0:T(8,128)(2,1)S(1)}, u32[]{:S(2)}, u32[]{:S(2)}) collective-permute-start(bf16[128,256]{1,0:T(8,128)(2,1)S(1)} %get-tuple-element.990), channel_id=1, source_target_pairs={{0,16},{16,32},{32,48},{48,64},{64,80},{80,96},{96,112},{112,128},... | collective-permute-start | bytes 196616 | tf_op jit(solution)/shard_map/while/body/eval_jaxpr/ppermute | solution.py:12
  83.7 5.9 collective-permute-start
  91.9 12.2 %collective-permute-start = (bf16[128,256]{1,0:T(8,128)(2,1)S(1)}, bf16[128,256]{1,0:T(8,128)(2,1)S(1)}, u32[]{:S(2)}, u32[]{:S(2)}) collective-permute-start(bf16[128,256]{1,0:T(8,128)(2,1)S(1)} %get-tuple-element.990), channel_id=1, source_target_pairs={{0,16},{16,32},{32,48},{48,64},{64,80},{80,96},{96,112},{112,128},... | collective-permute-start | bytes 196616 | tf_op jit(solution)/shard_map/while/body/eval_jaxpr/ppermute | solution.py:12
  106.4 5.9 collective-permute-start
  114.6 13.1 %collective-permute-start = (bf16[128,256]{1,0:T(8,128)(2,1)S(1)}, bf16[128,256]{1,0:T(8,128)(2,1)S(1)}, u32[]{:S(2)}, u32[]{:S(2)}) collective-permute-start(bf16[128,256]{1,0:T(8,128)(2,1)S(1)} %get-tuple-element.990), channel_id=1, source_target_pairs={{0,16},{16,32},{32,48},{48,64},{64,80},{80,96},{96,112},{112,128},... | collective-permute-start | bytes 196616 | tf_op jit(solution)/shard_map/while/body/eval_jaxpr/ppermute | solution.py:12
  130.0 5.9 collective-permute-start
  138.1 12.2 %collective-permute-start = (bf16[128,256]{1,0:T(8,128)(2,1)S(1)}, bf16[128,256]{1,0:T(8,128)(2,1)S(1)}, u32[]{:S(2)}, u32[]{:S(2)}) collective-permute-start(bf16[128,256]{1,0:T(8,128)(2,1)S(1)} %get-tuple-element.990), channel_id=1, source_target_pairs={{0,16},{16,32},{32,48},{48,64},{64,80},{80,96},{96,112},{112,128},... | collective-permute-start | bytes 196616 | tf_op jit(solution)/shard_map/while/body/eval_jaxpr/ppermute | solution.py:12
  152.6 5.9 collective-permute-start
  160.8 13.1 %collective-permute-start = (bf16[128,256]{1,0:T(8,128)(2,1)S(1)}, bf16[128,256]{1,0:T(8,128)(2,1)S(1)}, u32[]{:S(2)}, u32[]{:S(2)}) collective-permute-start(bf16[128,256]{1,0:T(8,128)(2,1)S(1)} %get-tuple-element.990), channel_id=1, source_target_pairs={{0,16},{16,32},{32,48},{48,64},{64,80},{80,96},{96,112},{112,128},... | collective-permute-start | bytes 196616 | tf_op jit(solution)/shard_map/while/body/eval_jaxpr/ppermute | solution.py:12
  176.2 5.9 collective-permute-start
  184.4 12.2 %collective-permute-start = (bf16[128,256]{1,0:T(8,128)(2,1)S(1)}, bf16[128,256]{1,0:T(8,128)(2,1)S(1)}, u32[]{:S(2)}, u32[]{:S(2)}) collective-permute-start(bf16[128,256]{1,0:T(8,128)(2,1)S(1)} %get-tuple-element.990), channel_id=1, source_target_pairs={{0,16},{16,32},{32,48},{48,64},{64,80},{80,96},{96,112},{112,128},... | collective-permute-start | bytes 196616 | tf_op jit(solution)/shard_map/while/body/eval_jaxpr/ppermute | solution.py:12
  198.9 5.9 collective-permute-start
  207.0 15.6 %collective-permute-start = (bf16[128,256]{1,0:T(8,128)(2,1)S(1)}, bf16[128,256]{1,0:T(8,128)(2,1)S(1)}, u32[]{:S(2)}, u32[]{:S(2)}) collective-permute-start(bf16[128,256]{1,0:T(8,128)(2,1)S(1)} %get-tuple-element.990), channel_id=1, source_target_pairs={{0,16},{16,32},{32,48},{48,64},{64,80},{80,96},{96,112},{112,128},... | collective-permute-start | bytes 196616 | tf_op jit(solution)/shard_map/while/body/eval_jaxpr/ppermute | solution.py:12
  225.1 7.4 collective-permute-start.1
  234.9 4.2 copy-start.3
  234.9 11.3 %collective-permute-start.1 = (bf16[128,256]{1,0:T(8,128)(2,1)}, bf16[128,256]{1,0:T(8,128)(2,1)S(1)}, u32[]{:S(2)}, u32[]{:S(2)}) collective-permute-start(bf16[128,256]{1,0:T(8,128)(2,1)} %get-tuple-element.1008), channel_id=1, source_target_pairs={{16,0},{32,16},{48,32},{64,48},{80,64},{96,80},{112,96},{128,112},... | collective-permute-start | bytes 196616 | tf_op jit(solution)/shard_map/while/body/eval_jaxpr/ppermute | solution.py:12
  239.3 6.8 copy-start.4
  240.5 5.7 copy-start.8
  248.6 4.2 copy-start.3
  248.6 8.1 collective-permute-start.1
  259.1 4.2 copy-start.3
  259.1 11.5 %collective-permute-start.1 = (bf16[128,256]{1,0:T(8,128)(2,1)}, bf16[128,256]{1,0:T(8,128)(2,1)S(1)}, u32[]{:S(2)}, u32[]{:S(2)}) collective-permute-start(bf16[128,256]{1,0:T(8,128)(2,1)} %get-tuple-element.1008), channel_id=1, source_target_pairs={{16,0},{32,16},{48,32},{64,48},{80,64},{96,80},{112,96},{128,112},... | collective-permute-start | bytes 196616 | tf_op jit(solution)/shard_map/while/body/eval_jaxpr/ppermute | solution.py:12
  263.6 7.1 copy-start.4
  264.7 5.9 copy-start.8
  273.1 4.2 copy-start.3
  273.1 8.6 collective-permute-start.1
  284.2 4.2 copy-start.3
  284.2 10.1 %collective-permute-start.1 = (bf16[128,256]{1,0:T(8,128)(2,1)}, bf16[128,256]{1,0:T(8,128)(2,1)S(1)}, u32[]{:S(2)}, u32[]{:S(2)}) collective-permute-start(bf16[128,256]{1,0:T(8,128)(2,1)} %get-tuple-element.1008), channel_id=1, source_target_pairs={{16,0},{32,16},{48,32},{64,48},{80,64},{96,80},{112,96},{128,112},... | collective-permute-start | bytes 196616 | tf_op jit(solution)/shard_map/while/body/eval_jaxpr/ppermute | solution.py:12
  288.6 5.6 copy-start.4
  289.8 4.5 copy-start.8
  296.7 4.2 copy-start.3
  296.7 7.2 collective-permute-start.1
  306.4 4.2 copy-start.3
  306.4 12.2 %collective-permute-start.1 = (bf16[128,256]{1,0:T(8,128)(2,1)}, bf16[128,256]{1,0:T(8,128)(2,1)S(1)}, u32[]{:S(2)}, u32[]{:S(2)}) collective-permute-start(bf16[128,256]{1,0:T(8,128)(2,1)} %get-tuple-element.1008), channel_id=1, source_target_pairs={{16,0},{32,16},{48,32},{64,48},{80,64},{96,80},{112,96},{128,112},... | collective-permute-start | bytes 196616 | tf_op jit(solution)/shard_map/while/body/eval_jaxpr/ppermute | solution.py:12
  310.8 7.8 copy-start.4
  312.0 6.6 copy-start.8
  321.1 7.4 collective-permute-start.1
  331.0 11.1 %collective-permute-start.1 = (bf16[128,256]{1,0:T(8,128)(2,1)}, bf16[128,256]{1,0:T(8,128)(2,1)S(1)}, u32[]{:S(2)}, u32[]{:S(2)}) collective-permute-start(bf16[128,256]{1,0:T(8,128)(2,1)} %get-tuple-element.1008), channel_id=1, source_target_pairs={{16,0},{32,16},{48,32},{64,48},{80,64},{96,80},{112,96},{128,112},... | collective-permute-start | bytes 196616 | tf_op jit(solution)/shard_map/while/body/eval_jaxpr/ppermute | solution.py:12
  335.4 6.7 copy-start.4
  336.6 5.5 copy-start.8
  344.6 4.2 copy-start.3
  344.6 8.3 collective-permute-start.1
  355.3 12.6 %collective-permute-start.1 = (bf16[128,256]{1,0:T(8,128)(2,1)}, bf16[128,256]{1,0:T(8,128)(2,1)S(1)}, u32[]{:S(2)}, u32[]{:S(2)}) collective-permute-start(bf16[128,256]{1,0:T(8,128)(2,1)} %get-tuple-element.1008), channel_id=1, source_target_pairs={{16,0},{32,16},{48,32},{64,48},{80,64},{96,80},{112,96},{128,112},... | collective-permute-start | bytes 196616 | tf_op jit(solution)/shard_map/while/body/eval_jaxpr/ppermute | solution.py:12
  359.7 8.2 copy-start.4
  360.9 7.0 copy-start.8
  370.4 6.9 collective-permute-start.1
  379.7 11.9 %collective-permute-start.1 = (bf16[128,256]{1,0:T(8,128)(2,1)}, bf16[128,256]{1,0:T(8,128)(2,1)S(1)}, u32[]{:S(2)}, u32[]{:S(2)}) collective-permute-start(bf16[128,256]{1,0:T(8,128)(2,1)} %get-tuple-element.1008), channel_id=1, source_target_pairs={{16,0},{32,16},{48,32},{64,48},{80,64},{96,80},{112,96},{128,112},... | collective-permute-start | bytes 196616 | tf_op jit(solution)/shard_map/while/body/eval_jaxpr/ppermute | solution.py:12
  384.2 7.4 copy-start.4
  385.3 6.3 copy-start.8
  394.1 223.6 %collective-permute-start.1 = (bf16[128,256]{1,0:T(8,128)(2,1)}, bf16[128,256]{1,0:T(8,128)(2,1)S(1)}, u32[]{:S(2)}, u32[]{:S(2)}) collective-permute-start(bf16[128,256]{1,0:T(8,128)(2,1)} %get-tuple-element.1008), channel_id=1, source_target_pairs={{16,0},{32,16},{48,32},{64,48},{80,64},{96,80},{112,96},{128,112},... | collective-permute-start | bytes 196616 | tf_op jit(solution)/shard_map/while/body/eval_jaxpr/ppermute | solution.py:12
  398.5 219.2 %copy-start.4 = (f32[1024,256]{1,0:T(8,128)}, f32[1024,256]{1,0:T(8,128)S(1)}, u32[]{:S(2)}) copy-start(f32[1024,256]{1,0:T(8,128)S(1)} %select_add_fusion.7) | copy-start | bytes 3145732 | tf_op jit(solution)/shard_map/while
  399.7 218.0 %copy-start.8 = (f32[4096]{0:T(1024)}, f32[4096]{0:T(1024)S(1)}, u32[]{:S(2)}) copy-start(f32[4096]{0:T(1024)S(1)} %select_add_fusion.8) | copy-start | bytes 49156 | tf_op jit(solution)/shard_map/while
  617.7 4.7 copy-start
  634.7 8.0 collective-permute-start.1
  642.7 4.7 copy-start
  659.8 5.6 collective-permute-start.1
  668.3 213.1 %reduce-scatter.3.cloned.1.call-start = ((), (), s32[]{:S(2)}) async-start(), calls=%async_computation.2 | async-start | bytes 8912896 | tf_op jit(solution)/shard_map/reduce_scatter | solution.py:178
  (51 other events, 113.2 us)
Sparse Core Ops, SparseCore 0:
  668.4 97.6 reduce-scatter.4
  771.4 109.9 reduce-scatter.2
where the time goes:
time: 896 us; the launch traced here: 890 us
  waiting for transfers between devices  403 us (45%)
  starting transfers between devices  151 us (17%)
  other arithmetic  127 us (14%)
  blocking collectives  66 us (7%)
  matrix products  65.5 us (7%)
  local copies, waits for them, and re-layouts  61.7 us (7%)
  between operations  14.8 us (2%)
    ppermute x34, waiting for transfers between devices, passed_along(): return lax.ppermute(value, axis, pairs)  277 us
    ppermute x34, starting transfers between devices, passed_along(): return lax.ppermute(value, axis, pairs)  151 us
    reduce_scatter x1, waiting for transfers between devices, shards(): lax.psum_scatter(partial_grad.astype(jnp.bfloat16), 'dp', scatter_dimensi...  114 us
    unnamed x1, blocking collectives  66 us
    add x17, other arithmetic, backward_turn(): factor_sum + factor  46.1 us
    another operation x77, local copies, waits for them, and re-layouts  36.8 us
    select_n x17, other arithmetic, forward_turn(): jnp.where(active, lax.dynamic_update_index_in_dim(saved_pooled, pooled, c...  29.7 us
    select_n x17, other arithmetic, forward_turn(): jnp.where(active, lax.dynamic_update_index_in_dim(saved_coeff, section_co...  25.9 us
  transfers between devices with their start and end apart: 36, of which 18 were waited for; matrix products, arithmetic and copies ran while one was open for 13% of the time, Pallas kernels for 0%

commit v1 on v0

v1 whole, which is shorter than its diff:
```python
import functools

import jax
import jax.numpy as jnp
from jax import lax
from jax.experimental import pallas as pl
from jax.experimental.pallas import tpu as pltpu
from jax.sharding import PartitionSpec as P

EPS = 1e-05
F32 = jnp.float32
BF16 = jnp.bfloat16


def mm(a, b, dims=((1,), (0,))):
    return lax.dot_general(a, b, (dims, ((), ())), preferred_element_type=F32)


def mixing_pair(seg_row):
    rows = seg_row.shape[1]
    across = jnp.broadcast_to(seg_row, (rows, rows))
    down = across.T
    i = lax.broadcasted_iota(jnp.int32, (rows, rows), 0)
    j = lax.broadcasted_iota(jnp.int32, (rows, rows), 1)
    same = across == down
    low = jnp.where(same & (j <= i), 1.0, 0.0).astype(F32)
    high = jnp.where(same & (i <= j), 1.0, 0.0).astype(F32)
    mixing = (low / jnp.sum(low, axis=1, keepdims=True)).astype(BF16)
    mixing_t = (high / jnp.sum(high, axis=0, keepdims=True)).astype(BF16)
    return mixing, mixing_t


def chain(width, n_ref, gram_ref, c_ref, cot_ref, seg_ref, f_ref, xs, ps, es, hs, invs):
    sections = n_ref.shape[0]
    micros = c_ref.shape[0]
    gram = gram_ref[...]
    gram_b = gram.astype(BF16)
    mixings = [mixing_pair(seg_ref[m : m + 1, :].astype(F32)) for m in range(micros)]
    cs = [c_ref[m].astype(F32) for m in range(micros)]
    hh = [mm(c_ref[m], gram_b) for m in range(micros)]
    for s in range(sections):
        n = n_ref[s]
        ng = mm(n, gram_b).astype(BF16)
        for m in range(micros):
            cb = cs[m].astype(BF16)
            ms = jnp.sum(cs[m] * hh[m], axis=1, keepdims=True) * (1.0 / width)
            inv = lax.rsqrt(jnp.maximum(ms, 0.0) + EPS)
            e = mm(cb, n)
            f = mm(cb, ng)
            xs[s, m] = (inv * cs[m]).astype(BF16)
            es[s, m] = e
            hs[s, m] = hh[m]
            invs[s, m] = jnp.broadcast_to(inv, invs.shape[2:])
            y = mm(mixings[m][0], (inv * e).astype(BF16))
            z = mm(mixings[m][0], (inv * f).astype(BF16))
            cs[m] = cs[m] + y
            hh[m] = hh[m] + z
    gs = [cot_ref[m].astype(F32) for m in range(micros)]
    for s in reversed(range(sections)):
        n = n_ref[s]
        for m in range(micros):
            p = mm(mixings[m][1], gs[m].astype(BF16))
            pb = p.astype(BF16)
            ps[s, m] = pb
            q = mm(pb, n, ((1,), (1,)))
            inv = invs[s, m][:, :1]
            t = jnp.sum(p * es[s, m], axis=1, keepdims=True)
            gs[m] = gs[m] + inv * q - (inv * inv * inv * t * (1.0 / width)) * hs[s, m]
    own = lax.axis_index("section")
    total = mm(xs[own, 0], ps[own, 0], ((0,), (0,)))
    for m in range(1, micros):
        total = total + mm(xs[own, m], ps[own, m], ((0,), (0,)))
    f_ref[...] = total


def run_chain(n_all, gram, coeffs, cotangent, segments, width):
    sections, sub, _ = n_all.shape
    micros, rows, _ = coeffs.shape
    whole = pl.BlockSpec(memory_space=pltpu.VMEM)
    return pl.pallas_call(
        functools.partial(chain, width),
        out_shape=jax.ShapeDtypeStruct((sub, sub), F32),
        in_specs=[whole] * 5,
        out_specs=whole,
        scratch_shapes=[
            pltpu.VMEM((sections, micros, rows, sub), BF16),
            pltpu.VMEM((sections, micros, rows, sub), BF16),
            pltpu.VMEM((sections, micros, rows, sub), F32),
            pltpu.VMEM((sections, micros, rows, sub), F32),
            pltpu.VMEM((sections, micros, rows, 128), F32),
        ],
        compiler_params=pltpu.CompilerParams(vmem_limit_bytes=48 * 1024 * 1024),
    )(n_all, gram, coeffs, cotangent, segments)


def shards(coeffs, cotangent, segment_ids, basis_matrix, section_gains, value_weight, out_weight):
    replicas = lax.axis_size("dp")
    replica = lax.axis_index("dp")
    gain = section_gains[0]
    value = value_weight[0]
    out = out_weight[0]
    width, inner = value.shape
    rows = width // replicas
    cols = inner // replicas
    scaled_basis = (gain[:, None] * basis_matrix.astype(F32)).astype(BF16)
    folded = mm(scaled_basis, value, ((0,), (0,))).astype(BF16)
    step = mm(folded, out).astype(BF16)
    steps = lax.all_gather(step, "section")
    gram = mm(basis_matrix, basis_matrix, ((0,), (0,)))
    factor_part = run_chain(steps, gram, coeffs, cotangent, segment_ids, width)
    factor = lax.psum(factor_part.astype(BF16), "dp")
    wide = mm(factor, out, ((1,), (1,))).astype(BF16)
    own_basis = lax.dynamic_slice_in_dim(basis_matrix, replica * rows, rows, 0)
    own_gain = lax.dynamic_slice_in_dim(gain, replica * rows, rows, 0)
    own_value = lax.dynamic_slice_in_dim(value, replica * rows, rows, 0)
    plain = mm(own_basis, wide)
    grad_value = own_gain[:, None] * plain
    grad_gain = jnp.sum(plain * own_value.astype(F32), axis=1)
    own_folded = lax.dynamic_slice_in_dim(folded, replica * cols, cols, 1)
    grad_out = mm(own_folded, factor, ((0,), (0,)))
    return (grad_value[None], grad_out[None], grad_gain[None])


def solution(mesh):
    placed = (
        P(None, "dp", None),
        P(None, "dp", None),
        P(None, "dp"),
        P(),
        P("section", None),
        P("section", None, None),
        P("section", None, None),
    )
    return jax.shard_map(
        shards,
        mesh=mesh,
        in_specs=placed,
        out_specs=(P("section", "dp", None), P("section", "dp", None), P("section", "dp")),
        check_vma=False,
    )
```

time: 896 us -> 261 us (0.29)
  waiting for transfers between devices: 403 us -> 215 us
  starting transfers between devices: 151 us -> 0.26 us
  other arithmetic: 127 us -> 0.67 us
  blocking collectives: 66 us -> 0 us
  local copies, waits for them, and re-layouts: 61.7 us -> 3.09 us
  matrix products: 65.5 us -> 13.4 us
  Pallas kernels: 0 us -> 14.7 us
    ppermute x34 -> x0, waiting for transfers between devices: 277 us -> none  [passed_along(): return lax.ppermute(value, axis, pairs)]
    ppermute x34 -> x0, starting transfers between devices: 151 us -> none  [passed_along(): return lax.ppermute(value, axis, pairs)]
    psum x0 -> x1, waiting for transfers between devices: none -> 148 us  [shards(): factor = lax.psum(factor_part.astype(BF16), 'dp')]
    reduce_scatter x2 -> x0, waiting for transfers between devices: 126 us -> none  [the longest x1 114 us: shards(): lax.psum_scatter(partial_grad.astype(jnp.bfloat16), 'dp', scatter_dimensi...]
    all_gather x0 -> x1, waiting for transfers between devices: none -> 66.8 us  [shards(): steps = lax.all_gather(step, 'section')]
    unnamed x1 -> x0, blocking collectives: 66 us -> none
    add x51 -> x0, other arithmetic: 63 us -> none  [the longest x17 46.1 us: backward_turn(): factor_sum + factor]
    select_n x36 -> x0, other arithmetic: 57.2 us -> none  [the longest x17 29.7 us: forward_turn(): jnp.where(active, lax.dynamic_update_index_in_dim(saved_pooled, pooled, c...]
  transfers between devices with their start and end apart: 36 -> 2, of which waited for: 18 -> 2; matrix products, arithmetic and copies ran while one was open for 13% -> 1% of each run, Pallas kernels for 0% -> 0%
where the time goes in v1:
time: 261 us
  waiting for transfers between devices  215 us (82%)
  Pallas kernels  14.7 us (6%)
  between operations  14.1 us (5%)
  matrix products  13.4 us (5%)
  local copies, waits for them, and re-layouts  3.09 us (1%)
    psum x1, waiting for transfers between devices, shards(): factor = lax.psum(factor_part.astype(BF16), 'dp')  148 us
    all_gather x1, waiting for transfers between devices, shards(): steps = lax.all_gather(step, 'section')  66.8 us
    pallas_call x1, Pallas kernels, run_chain(): pl.pallas_call(functools.partial(chain, width), out_shape=jax.ShapeDtypeS...  14.7 us
    dot_general x5, matrix products, mm(): return lax.dot_general(a, b, (dims, ((), ())), preferred_element_type=F32)  13.4 us
  transfers between devices with their start and end apart: 2, of which 2 were waited for; matrix products, arithmetic and copies ran while one was open for 1% of the time, Pallas kernels for 0%

profile of v1, /device:TPU:1, one launch (start us, length us, event | category | flops | bytes accessed | tf_op | source)
XLA Modules:
  0.0 261.2 jit_solution(12666474585065234241)
XLA Ops:
  7.2 0.0 copy-start
  7.2 0.0 all-gather.3.cloned.1.call-start
  7.2 0.0 copy-start.5
  7.2 6.6 %fusion.3 = bf16[256,1024]{1,0:T(8,128)(2,1)S(1)} fusion(bf16[1,4096,1024]{2,1,0:T(8,128)(2,1)} %param.12, bf16[4096,256]{1,0:T(8,128)(2,1)} %param.10, f32[4096]{0:T(1024)} %bitcast.30), kind=kOutput, calls=%fused_computation.4 | convolution fusion | flops 2150891520 | bytes 11026432 | tf_op jit(solution)/shard_map/dot_general | solution.py:16
  13.9 0.0 copy-start.6
  13.9 0.8 copy-done.6
  14.7 0.0 copy-done
  14.7 1.0 convolution_convert_fusion.1
  15.6 0.0 all-gather.3.cloned.1.call-update
  15.7 0.0 copy-start.2
  15.7 0.0 copy-start.3
  15.7 0.0 copy-start.4
  15.7 0.2 all-reduce.2.cloned.1.call-start
  15.9 0.0 copy-done.5
  15.9 0.7 fusion.19.gram_ref
  16.7 66.8 %all-gather.3.cloned.1.call-done = bf16[4096,256]{1,0:T(8,128)(2,1)} async-done(((bf16[256,256]{1,0:T(8,128)(2,1)}), bf16[4096,256]{1,0:T(8,128)(2,1)}) %all-gather.3.cloned.1.call-update) | async-done | bytes 2097168 | tf_op jit(solution)/shard_map/all_gather | solution.py:108
  83.4 0.0 copy-done.2
  83.4 0.0 copy-done.3
  83.4 0.0 copy-done.4
  83.4 0.0 copy-start.1
  83.5 1.6 copy-done.1
  85.0 14.7 %shard_map.94 = f32[256,256]{1,0:T(8,128)S(1)} custom-call(bf16[16,256,256]{2,1,0:T(8,128)(2,1)S(1)} %bitcast.29, f32[256,256]{1,0:T(8,128)S(1)} %fusion.19.gram_ref, bf16[2,128,256]{2,1,0:T(8,128)(2,1)S(1)} %copy-done.2, bf16[2,128,256]{2,1,0:T(8,128)(2,1)S(1)} %copy-done.3, s32[2,128]{1,0:T(2,128)S(1)} %copy-done.4), custom_call_target="tpu_custom_call" | custom-call | tf_op jit(solution)/shard_map/pallas_call | solution.py:80
  99.7 0.7 convert_element_type.28
  100.4 0.0 all-reduce.2.cloned.1.call-update
  100.5 0.7 constant_dynamic-slice_fusion
  101.1 148.1 %all-reduce.2.cloned.1.call-done = bf16[256,256]{1,0:T(8,128)(2,1)} async-done(((bf16[256,256]{1,0:T(8,128)(2,1)}), bf16[256,256]{1,0:T(8,128)(2,1)}) %all-reduce.2.cloned.1.call-update) | async-done | bytes 131088 | tf_op jit(solution)/shard_map/psum | solution.py:111
  249.3 1.8 convolution_bitcast_fusion
  251.1 3.3 %fusion.7 = (f32[256]{0:T(256)}, f32[1,256,1024]{2,1,0:T(8,128)}) fusion(bf16[1,4096,1024]{2,1,0:T(8,128)(2,1)} %param.12, s32[]{:T(128)S(6)} %select_n.8, f32[256]{0:T(256)S(1)} %bitcast.31, bf16[256,256]{1,0:T(8,128)(2,1)} %all-reduce.2.cloned.1.call-done, bf16[1,1024,256]{2,1,0:T(8,128)(2,1)S(1)} %copy-done, bf16[4096,256]{1,0:T(8,128)(2,1)S(1)} %copy-done.5), kind=kOutput, calls=%fused_computation.10 | convolution fusion | flops 269745920 | bytes 2362368 | tf_op jit(solution)/shard_map/dot_general | solution.py:16
Async XLA Ops:
  7.2 7.5 %copy-start = (bf16[1,1024,256]{2,1,0:T(8,128)(2,1)S(1)}, bf16[1,1024,256]{2,1,0:T(8,128)(2,1)}, u32[]{:S(2)}) copy-start(bf16[1,1024,256]{2,1,0:T(8,128)(2,1)} %param.13) | copy-start | bytes 1572868
  7.2 76.3 %all-gather.3.cloned.1.call-start = ((), (), s32[]{:S(2)}) async-start(), calls=%async_computation.1 | async-start | bytes 2228224 | tf_op jit(solution)/shard_map/all_gather | solution.py:108
  7.2 8.7 %copy-start.5 = (bf16[4096,256]{1,0:T(8,128)(2,1)S(1)}, bf16[4096,256]{1,0:T(8,128)(2,1)}, u32[]{:S(2)}) copy-start(bf16[4096,256]{1,0:T(8,128)(2,1)} %param.10) | copy-start | bytes 6291460
  13.9 0.8 copy-start.6
  15.7 67.8 %copy-start.2 = (bf16[2,128,256]{2,1,0:T(8,128)(2,1)S(1)}, bf16[2,128,256]{2,1,0:T(8,128)(2,1)}, u32[]{:S(2)}) copy-start(bf16[2,128,256]{2,1,0:T(8,128)(2,1)} %c_ref.1) | copy-start | bytes 393220
  15.7 67.8 %copy-start.3 = (bf16[2,128,256]{2,1,0:T(8,128)(2,1)S(1)}, bf16[2,128,256]{2,1,0:T(8,128)(2,1)}, u32[]{:S(2)}) copy-start(bf16[2,128,256]{2,1,0:T(8,128)(2,1)} %cot_ref.1) | copy-start | bytes 393220
  15.7 67.8 %copy-start.4 = (s32[2,128]{1,0:T(2,128)S(1)}, s32[2,128]{1,0:T(2,128)}, u32[]{:S(2)}) copy-start(s32[2,128]{1,0:T(2,128)} %seg_ref.1) | copy-start | bytes 3076
  15.7 233.6 %all-reduce.2.cloned.1.call-start = ((), (), s32[]{:S(2)}) async-start(), calls=%async_computation | async-start | bytes 262144 | tf_op jit(solution)/shard_map/psum | solution.py:111
  83.4 1.6 copy-start.1
Sparse Core Ops, SparseCore 0:
  15.8 67.6 all-gather.2
  100.6 148.6 all-reduce.1

commit v2 on v1

--- a/solution.py
+++ b/solution.py
@@ -8,6 +8,7 @@
 from jax.sharding import PartitionSpec as P
 
 EPS = 1e-05
+MESH = pl.DeviceIdType.MESH
 F32 = jnp.float32
 BF16 = jnp.bfloat16
 
@@ -30,8 +31,204 @@
     return mixing, mixing_t
 
 
+class Place:
+    def __init__(self):
+        self.s = lax.axis_index("section")
+        self.d = lax.axis_index("dp")
+        self.z = self.s // 2
+        self.xl = self.s % 2
+        self.y = self.d // 4
+        self.xh = (self.d // 2) % 2
+        self.core = self.d % 2
+        self.x = self.xh * 2 + self.xl
+
+    def dp_peer(self, k):
+        return (self.s, (self.d + k) % 16)
+
+    def z_peer(self, k):
+        return (((self.z + k) % 8) * 2 + self.xl, self.d)
+
+    def y_peer(self, k):
+        return (self.s, ((self.y + k) % 4) * 4 + self.xh * 2 + self.core)
+
+    def x_peer(self, k):
+        x = (self.x + k) % 4
+        return (self.z * 2 + x % 2, self.y * 4 + (x // 2) * 2 + self.core)
+
+    def core_peer(self):
+        return (self.s, self.y * 4 + self.xh * 2 + (self.core + 1) % 2)
+
+
+def piece_of(d):
+    return (d % 2) * 8 + d // 2
+
+
+def greet(peers):
+    barrier = pltpu.get_barrier_semaphore()
+    for peer in peers:
+        pl.semaphore_signal(barrier, inc=1, device_id=peer, device_id_type=MESH)
+    pl.semaphore_wait(barrier, len(peers))
+
+
+def send(src, dst, send_sem, recv_sem, peer):
+    copy = pltpu.make_async_remote_copy(
+        src_ref=src, dst_ref=dst, send_sem=send_sem, recv_sem=recv_sem,
+        device_id=peer, device_id_type=MESH,
+    )
+    copy.start()
+    return copy
+
+
+def reduce_pieces(at, part, part_b, slots, send_sem, recv_sem):
+    part_b[...] = part[...].astype(BF16)
+    copies = []
+    for k in range(1, 16):
+        copies.append(
+            send(part_b.at[piece_of((at.d + k) % 16)], slots.at[k], send_sem.at[k], recv_sem.at[k], at.dp_peer(k))
+        )
+    total = part[piece_of(at.d)]
+    for k in range(1, 16):
+        copies[k - 1].wait_recv()
+        total = total + slots[k].astype(F32)
+    for copy in copies:
+        copy.wait_send()
+    return total
+
+
+def fold_and_gather(
+    basis_hbm, gain_ref, value_hbm, out_hbm, all_ref, gram_ref, folded_ref,
+    basis, basis_own, value_own, value_cols, out, gain_pad, part, part_b, slots,
+    load_sem, rs_send, rs_recv, z_send, z_recv, h0_send, h0_recv, h1_send, h1_recv, c_send, c_recv,
+):
+    at = Place()
+    rows = pl.ds(pl.multiple_of(at.d * 256, 256), 256)
+    cols = pl.ds(pl.multiple_of((at.d // 2) * 128, 128), 128)
+    loads = [
+        pltpu.make_async_copy(value_hbm.at[0, rows, :], value_own, load_sem.at[0]),
+        pltpu.make_async_copy(out_hbm.at[0], out, load_sem.at[1]),
+        pltpu.make_async_copy(basis_hbm.at[rows, :], basis_own, load_sem.at[2]),
+        pltpu.make_async_copy(basis_hbm, basis, load_sem.at[3]),
+        pltpu.make_async_copy(value_hbm.at[0, :, cols], value_cols, load_sem.at[4]),
+    ]
+    for load in loads:
+        load.start()
+    peers = [at.dp_peer(k) for k in range(1, 16)] + [at.z_peer(k) for k in range(1, 8)]
+    peers += [at.x_peer(1), at.x_peer(3)]
+    greet(peers)
+    gain_pad[...] = jnp.zeros_like(gain_pad)
+    gain_pad[0:16, :] = gain_ref[...]
+    gain_cols = gain_pad[...].T
+    lane = lax.broadcasted_iota(jnp.int32, gain_cols.shape, 1)
+    own_gain = jnp.sum(jnp.where(lane == at.d, gain_cols, 0.0), axis=1, keepdims=True)
+    loads[0].wait()
+    loads[1].wait()
+    through = mm(value_own[...], out[...]).astype(BF16)
+    loads[2].wait()
+    scaled = (basis_own[...].astype(F32) * own_gain).astype(BF16)
+    part[...] = mm(scaled, through, ((0,), (0,))).reshape(16, 16, 256)
+    piece = reduce_pieces(at, part, part_b, slots, rs_send, rs_recv)
+
+    own = all_ref.at[at.core, at.z % 2, at.y, at.xh, at.xl, at.z // 2]
+    own[...] = piece.astype(BF16)
+    over_z = [send(own, own, z_send.at[k], z_recv.at[k], at.z_peer(k)) for k in range(1, 8)]
+
+    loads[3].wait()
+    loads[4].wait()
+    gram = jnp.zeros((256, 256), F32)
+    folded = jnp.zeros((256, 128), F32)
+    for i in range(16):
+        chunk = basis[i * 256 : (i + 1) * 256, :]
+        gram = gram + mm(chunk, chunk, ((0,), (0,)))
+        scaled = (chunk.astype(F32) * gain_cols[:, i : i + 1]).astype(BF16)
+        folded = folded + mm(scaled, value_cols[i * 256 : (i + 1) * 256, :], ((0,), (0,)))
+    gram_ref[...] = gram
+    folded_ref[...] = folded.astype(BF16)
+
+    for copy in over_z:
+        copy.wait_recv()
+    own0 = all_ref.at[at.core, 0, at.y, at.xh, at.xl]
+    own1 = all_ref.at[at.core, 1, at.y, at.xh, at.xl]
+    x0 = [send(own0, own0, h0_send.at[k], h0_recv.at[k], at.x_peer(k)) for k in range(1, 4)]
+    y1 = [send(own1, own1, h1_send.at[k], h1_recv.at[k], at.y_peer(k)) for k in range(1, 4)]
+    for copy in x0:
+        copy.wait_recv()
+    row0 = all_ref.at[at.core, 0, at.y]
+    y0 = [send(row0, row0, h0_send.at[3 + k], h0_recv.at[3 + k], at.y_peer(k)) for k in range(1, 4)]
+    for copy in y1:
+        copy.wait_recv()
+    row1 = all_ref.at[at.core, 1, :, at.xh, at.xl]
+    x1 = [send(row1, row1, h1_send.at[3 + k], h1_recv.at[3 + k], at.x_peer(k)) for k in range(1, 4)]
+    for copy in y0 + x1:
+        copy.wait_recv()
+    half = all_ref.at[at.core]
+    across = send(half, half, c_send, c_recv, at.core_peer())
+    across.wait_recv()
+    for copy in over_z + x0 + y1 + y0 + x1 + [across]:
+        copy.wait_send()
+
+
+def run_fold(basis, gain, value, out):
+    vmem = pl.BlockSpec(memory_space=pltpu.VMEM)
+    anywhere = pl.BlockSpec(memory_space=pl.ANY)
+    dma = pltpu.SemaphoreType.DMA
+    return pl.pallas_call(
+        fold_and_gather,
+        out_shape=(
+            jax.ShapeDtypeStruct((2, 2, 4, 2, 2, 4, 16, 256), BF16),
+            jax.ShapeDtypeStruct((256, 256), F32),
+            jax.ShapeDtypeStruct((256, 128), BF16),
+        ),
+        in_specs=[anywhere, vmem, anywhere, anywhere],
+        out_specs=(vmem, vmem, vmem),
+        scratch_shapes=[
+            pltpu.VMEM((4096, 256), BF16),
+            pltpu.VMEM((256, 256), BF16),
+            pltpu.VMEM((256, 1024), BF16),
+            pltpu.VMEM((4096, 128), BF16),
+            pltpu.VMEM((1024, 256), BF16),
+            pltpu.VMEM((128, 256), F32),
+            pltpu.VMEM((16, 16, 256), F32),
+            pltpu.VMEM((16, 16, 256), BF16),
+            pltpu.VMEM((16, 16, 256), BF16),
+            dma((5,)), dma((16,)), dma((16,)), dma((8,)), dma((8,)),
+            dma((7,)), dma((7,)), dma((7,)), dma((7,)), dma, dma,
+        ],
+        compiler_params=pltpu.CompilerParams(
+            collective_id=0, has_side_effects=True, vmem_limit_bytes=40 * 1024 * 1024
+        ),
+    )(basis, gain, value, out)
+
+
+def sum_factor(part_ref, whole_ref, part_b, slots, rs_send, rs_recv, ag_send, ag_recv):
+    at = Place()
+    greet([at.dp_peer(k) for k in range(1, 16)])
+    piece = reduce_pieces(at, part_ref, part_b, slots, rs_send, rs_recv)
+    own = whole_ref.at[piece_of(at.d)]
+    own[...] = piece.astype(BF16)
+    copies = [send(own, own, ag_send.at[k], ag_recv.at[k], at.dp_peer(k)) for k in range(1, 16)]
+    for copy in copies:
+        copy.wait()
+
+
+def run_sum(part):
+    vmem = pl.BlockSpec(memory_space=pltpu.VMEM)
+    dma = pltpu.SemaphoreType.DMA
+    return pl.pallas_call(
+        sum_factor,
+        out_shape=jax.ShapeDtypeStruct((16, 16, 256), BF16),
+        in_specs=[vmem],
+        out_specs=vmem,
+        scratch_shapes=[
+            pltpu.VMEM((16, 16, 256), BF16),
+            pltpu.VMEM((16, 16, 256), BF16),
+            dma((16,)), dma((16,)), dma((16,)), dma((16,)),
+        ],
+        compiler_params=pltpu.CompilerParams(collective_id=1, has_side_effects=True),
+    )(part)
+
+
 def chain(width, n_ref, gram_ref, c_ref, cot_ref, seg_ref, f_ref, xs, ps, es, hs, invs):
-    sections = n_ref.shape[0]
+    sections = 16
     micros = c_ref.shape[0]
     gram = gram_ref[...]
     gram_b = gram.astype(BF16)
@@ -39,7 +236,7 @@
     cs = [c_ref[m].astype(F32) for m in range(micros)]
     hh = [mm(c_ref[m], gram_b) for m in range(micros)]
     for s in range(sections):
-        n = n_ref[s]
+        n = step_of(n_ref, s)
         ng = mm(n, gram_b).astype(BF16)
         for m in range(micros):
             cb = cs[m].astype(BF16)
@@ -57,7 +254,7 @@
             hh[m] = hh[m] + z
     gs = [cot_ref[m].astype(F32) for m in range(micros)]
     for s in reversed(range(sections)):
-        n = n_ref[s]
+        n = step_of(n_ref, s)
         for m in range(micros):
             p = mm(mixings[m][1], gs[m].astype(BF16))
             pb = p.astype(BF16)
@@ -73,8 +270,13 @@
     f_ref[...] = total
 
 
+def step_of(n_ref, s):
+    z, xl = s // 2, s % 2
+    return n_ref[:, z % 2, :, :, xl, z // 2].reshape(256, 256)
+
+
 def run_chain(n_all, gram, coeffs, cotangent, segments, width):
-    sections, sub, _ = n_all.shape
+    sections, sub = 16, 256
     micros, rows, _ = coeffs.shape
     whole = pl.BlockSpec(memory_space=pltpu.VMEM)
     return pl.pallas_call(
@@ -93,32 +295,70 @@
     )(n_all, gram, coeffs, cotangent, segments)
 
 
+def finish(factor_ref, folded_ref, gain_ref, basis_hbm, value_hbm, out_hbm, gv_ref, go_ref, gg_ref,
+           basis, value, out, gain_pad, go_wide, load_sem):
+    d = lax.axis_index("dp")
+    rows = pl.ds(pl.multiple_of(d * 256, 256), 256)
+    loads = [
+        pltpu.make_async_copy(out_hbm.at[0], out, load_sem.at[0]),
+        pltpu.make_async_copy(basis_hbm.at[rows, :], basis, load_sem.at[1]),
+        pltpu.make_async_copy(value_hbm.at[0, rows, :], value, load_sem.at[2]),
+    ]
+    for load in loads:
+        load.start()
+    factor = factor_ref[...].reshape(256, 256)
+    go_wide[...] = mm(folded_ref[...], factor, ((0,), (0,)))
+    go_ref[0] = go_wide[pl.ds(pl.multiple_of((d % 2) * 64, 64), 64), :]
+    gain_pad[...] = jnp.zeros_like(gain_pad)
+    gain_pad[0:16, :] = gain_ref[...]
+    gain_cols = gain_pad[...].T
+    lane = lax.broadcasted_iota(jnp.int32, gain_cols.shape, 1)
+    own_gain = jnp.sum(jnp.where(lane == d, gain_cols, 0.0), axis=1, keepdims=True)
+    loads[0].wait()
+    loads[1].wait()
+    left = mm(basis[...], factor).astype(BF16)
+    plain = mm(left, out[...], ((1,), (1,)))
+    gv_ref[0] = own_gain * plain
+    loads[2].wait()
+    sums = jnp.sum(plain * value[...].astype(F32), axis=1, keepdims=True)
+    gg_ref[...] = jnp.broadcast_to(sums, (256, 128)).T[0:1, :]
+
+
+def run_finish(factor, folded, gain, basis, value, out):
+    vmem = pl.BlockSpec(memory_space=pltpu.VMEM)
+    anywhere = pl.BlockSpec(memory_space=pl.ANY)
+    return pl.pallas_call(
+        finish,
+        out_shape=(
+            jax.ShapeDtypeStruct((1, 256, 1024), F32),
+            jax.ShapeDtypeStruct((1, 64, 256), F32),
+            jax.ShapeDtypeStruct((1, 256), F32),
+        ),
+        in_specs=[vmem, vmem, vmem, anywhere, anywhere, anywhere],
+        out_specs=(vmem, vmem, vmem),
+        scratch_shapes=[
+            pltpu.VMEM((256, 256), BF16),
+            pltpu.VMEM((256, 1024), BF16),
+            pltpu.VMEM((1024, 256), BF16),
+            pltpu.VMEM((128, 256), F32),
+            pltpu.VMEM((128, 256), F32),
+            pltpu.SemaphoreType.DMA((3,)),
+        ],
+        compiler_params=pltpu.CompilerParams(vmem_limit_bytes=24 * 1024 * 1024),
+    )(factor, folded, gain, basis, value, out)
+
+
 def shards(coeffs, cotangent, segment_ids, basis_matrix, section_gains, value_weight, out_weight):
-    replicas = lax.axis_size("dp")
-    replica = lax.axis_index("dp")
-    gain = section_gains[0]
-    value = value_weight[0]
-    out = out_weight[0]
-    width, inner = value.shape
-    rows = width // replicas
-    cols = inner // replicas
-    scaled_basis = (gain[:, None] * basis_matrix.astype(F32)).astype(BF16)
-    folded = mm(scaled_basis, value, ((0,), (0,))).astype(BF16)
-    step = mm(folded, out).astype(BF16)
-    steps = lax.all_gather(step, "section")
-    gram = mm(basis_matrix, basis_matrix, ((0,), (0,)))
-    factor_part = run_chain(steps, gram, coeffs, cotangent, segment_ids, width)
-    factor = lax.psum(factor_part.astype(BF16), "dp")
-    wide = mm(factor, out, ((1,), (1,))).astype(BF16)
-    own_basis = lax.dynamic_slice_in_dim(basis_matrix, replica * rows, rows, 0)
-    own_gain = lax.dynamic_slice_in_dim(gain, replica * rows, rows, 0)
-    own_value = lax.dynamic_slice_in_dim(value, replica * rows, rows, 0)
-    plain = mm(own_basis, wide)
-    grad_value = own_gain[:, None] * plain
-    grad_gain = jnp.sum(plain * own_value.astype(F32), axis=1)
-    own_folded = lax.dynamic_slice_in_dim(folded, replica * cols, cols, 1)
-    grad_out = mm(own_folded, factor, ((0,), (0,)))
-    return (grad_value[None], grad_out[None], grad_gain[None])
+    width = basis_matrix.shape[0]
+    gain = section_gains.reshape(16, 256)
+    steps, gram, folded = run_fold(basis_matrix, gain, value_weight, out_weight)
+    part = run_chain(steps, gram, coeffs, cotangent, segment_ids, width)
+    order = jnp.reshape(part, (16, 16, 256))
+    factor = run_sum(order)
+    grad_value, grad_out, grad_gain = run_finish(
+        factor, folded, gain, basis_matrix, value_weight, out_weight
+    )
+    return (grad_value, grad_out, grad_gain)
 
 
 def solution(mesh):

time: 261 us -> 83.1 us (0.32)
  waiting for transfers between devices: 215 us -> 0 us
  Pallas kernels: 14.7 us -> 68.9 us
  matrix products: 13.4 us -> 0 us
  between operations: 14.1 us -> 0.91 us
  local copies, waits for them, and re-layouts: 3.09 us -> 11.5 us
    psum x1 -> x0, waiting for transfers between devices: 148 us -> none  [shards(): factor = lax.psum(factor_part.astype(BF16), 'dp')]
    all_gather x1 -> x0, waiting for transfers between devices: 66.8 us -> none  [shards(): steps = lax.all_gather(step, 'section')]
    pallas_call x0 -> x3, Pallas kernels: none -> 54.1 us  [the longest x1 37.2 us: run_fold(): pl.pallas_call(fold_and_gather, out_shape=(jax.ShapeDtypeStruct((2, 2, 4,...]
    dot_general x5 -> x0, matrix products: 13.4 us -> none  [mm(): return lax.dot_general(a, b, (dims, ((), ())), preferred_element_type=F32)]
    unnamed x14 -> x23, local copies, waits for them, and re-layouts: 2.41 us -> 11.5 us
  transfers between devices with their start and end apart: 2 -> 0, of which waited for: 2 -> 0; matrix products, arithmetic and copies ran while one was open for 1% -> 0% of each run, Pallas kernels for 0% -> 0%
where the time goes in v2:
time: 83.1 us; the launch traced here: 82.8 us
  Pallas kernels  68.9 us (83%)
  local copies, waits for them, and re-layouts  11.5 us (14%)
  other arithmetic  1.4 us (2%)
  between operations  0.91 us (1%)
    pallas_call x1, Pallas kernels, run_fold(): pl.pallas_call(fold_and_gather, out_shape=(jax.ShapeDtypeStruct((2, 2, 4,...  37.2 us
    pallas_call x1, Pallas kernels, run_sum(): pl.pallas_call(sum_factor, out_shape=jax.ShapeDtypeStruct((16, 16, 256),...  15 us
    pallas_call x1, Pallas kernels, run_chain(): pl.pallas_call(functools.partial(chain, width), out_shape=jax.ShapeDtypeS...  14.9 us
    unnamed x23, local copies, waits for them, and re-layouts  11.5 us
    pallas_call x1, Pallas kernels, run_finish(): pl.pallas_call(finish, out_shape=(jax.ShapeDtypeStruct((1, 256, 1024), F3...  1.91 us

profile of v2, /device:TPU:1, one launch (start us, length us, event | category | flops | bytes accessed | tf_op | source)
XLA Modules:
  0.0 82.8 jit_solution(7009659581053511607)
XLA Ops:
  0.6 0.5 broadcast.3
  1.1 1.4 %reduce.3 = f32[4096]{0:T(1024)S(1)} reduce(f32[1,4096]{1,0:T(1,128)} %param.11, f32[]{:T(128)} %broadcast.3), dimensions={0}, to_apply=%param.11.reduce_sub_computation.3 | reduce | bytes 32772 | tf_op args[4]
  2.6 0.0 copy-start
  2.6 3.4 %copy-done = bf16[1,4096,1024]{2,1,0:T(8,128)(2,1)S(1)} copy-done((bf16[1,4096,1024]{2,1,0:T(8,128)(2,1)S(1)}, bf16[1,4096,1024]{2,1,0:T(8,128)(2,1)}, u32[]{:S(2)}) %copy-start) | copy-done | bytes 8388632
  5.9 0.0 copy-start.2
  5.9 1.6 %copy-done.2 = bf16[4096,256]{1,0:T(8,128)(2,1)S(1)} copy-done((bf16[4096,256]{1,0:T(8,128)(2,1)S(1)}, bf16[4096,256]{1,0:T(8,128)(2,1)}, u32[]{:S(2)}) %copy-start.2) | copy-done | bytes 2097176
  7.5 0.0 copy-start.4
  7.5 1.0 %copy-done.4 = bf16[1,1024,256]{2,1,0:T(8,128)(2,1)S(1)} copy-done((bf16[1,1024,256]{2,1,0:T(8,128)(2,1)S(1)}, bf16[1,1024,256]{2,1,0:T(8,128)(2,1)}, u32[]{:S(2)}) %copy-start.4) | copy-done | bytes 524312
  8.6 0.0 copy-start.8
  8.6 0.0 copy-start.9
  8.6 0.0 copy-start.10
  8.6 37.2 %shard_map.94 = (bf16[2,2,4,2,2,4,16,256]{7,6,5,4,3,2,1,0:T(8,128)(2,1)S(1)}, f32[256,256]{1,0:T(8,128)S(1)}, bf16[256,128]{1,0:T(8,128)(2,1)S(1)}) custom-call(bf16[4096,256]{1,0:T(8,128)(2,1)S(1)} %copy-done.2, f32[16,256]{1,0:T(8,128)S(1)} %reshape.12.gain_ref, bf16[1,4096,1024]{2,1,0:T(8,128)(2,1)S(1)} %copy-done, bf16[1,1024,256]{2,1,0:T(8,128)(2,1)S(1)} %copy-done.4), custom_call_target="tpu_custom_call" | custom-call | tf_op jit(solution)/shard_map/pallas_call | solution.py:174
  45.8 0.0 copy-start.3
  45.8 0.0 copy-start.5
  45.8 0.0 copy-done.8
  45.8 0.0 copy-done.9
  45.8 0.0 copy-done.10
  45.8 14.9 %shard_map.95 = f32[256,256]{1,0:T(8,128)S(1)} custom-call(bf16[2,2,4,2,2,4,16,256]{7,6,5,4,3,2,1,0:T(8,128)(2,1)S(1)} %get-tuple-element.6.n_ref, f32[256,256]{1,0:T(8,128)S(1)} %get-tuple-element.7.gram_ref, bf16[2,128,256]{2,1,0:T(8,128)(2,1)S(1)} %copy-done.8, bf16[2,128,256]{2,1,0:T(8,128)(2,1)S(1)} %copy-done.9, s32[2,128]{1,0:T(2,128)S(1)} %copy-done.10), custom_call_target="tpu_custom_call" | custom-call | tf_op jit(solution)/shard_map/pallas_call | solution.py:282
  60.7 0.0 copy-start.6
  60.7 0.7 copy-done.6
  61.4 15.0 %shard_map.96.factor_ref = bf16[16,16,256]{2,1,0:T(8,128)(2,1)} custom-call(f32[16,16,256]{2,1,0:T(8,128)} %bitcast.1), custom_call_target="tpu_custom_call" | custom-call | tf_op jit(solution)/shard_map/pallas_call | solution.py:216
  76.4 0.0 copy-done.3
  76.4 0.0 copy-done.5
  76.4 0.0 copy-start.1
  76.4 3.4 %copy-done.1 = bf16[1,4096,1024]{2,1,0:T(8,128)(2,1)S(1)} copy-done((bf16[1,4096,1024]{2,1,0:T(8,128)(2,1)S(1)}, bf16[1,4096,1024]{2,1,0:T(8,128)(2,1)}, u32[]{:S(2)}) %copy-start.1) | copy-done | bytes 8388632
  79.8 0.0 copy-start.7
  79.8 0.9 %copy-done.7 = bf16[16,16,256]{2,1,0:T(8,128)(2,1)S(1)} copy-done((bf16[16,16,256]{2,1,0:T(8,128)(2,1)S(1)}, bf16[16,16,256]{2,1,0:T(8,128)(2,1)}, u32[]{:S(2)}) %copy-start.7) | copy-done | bytes 131096
  80.7 1.9 %shard_map.97 = (f32[1,256,1024]{2,1,0:T(8,128)}, f32[1,64,256]{2,1,0:T(8,128)}, f32[1,256]{1,0:T(1,128)}) custom-call(bf16[16,16,256]{2,1,0:T(8,128)(2,1)S(1)} %copy-done.7, bf16[256,128]{1,0:T(8,128)(2,1)S(1)} %get-tuple-element.8.folded_ref, f32[16,256]{1,0:T(8,128)S(1)} %reshape.12.gain_ref, bf16[4096,256]{1,0:T(8,128)(2,1)S(1)} %copy-done.3, ...), custom_call_target="tpu_custom_call" | custom-call | tf_op jit(solution)/shard_map/pallas_call | solution.py:330
  (1 shorter events, 0.0 us)
Async XLA Ops:
  2.6 3.4 %copy-start = (bf16[1,4096,1024]{2,1,0:T(8,128)(2,1)S(1)}, bf16[1,4096,1024]{2,1,0:T(8,128)(2,1)}, u32[]{:S(2)}) copy-start(bf16[1,4096,1024]{2,1,0:T(8,128)(2,1)} %value_hbm.3) | copy-start | bytes 25165828
  5.9 1.6 %copy-start.2 = (bf16[4096,256]{1,0:T(8,128)(2,1)S(1)}, bf16[4096,256]{1,0:T(8,128)(2,1)}, u32[]{:S(2)}) copy-start(bf16[4096,256]{1,0:T(8,128)(2,1)} %basis_hbm.3) | copy-start | bytes 6291460
  7.5 1.0 %copy-start.4 = (bf16[1,1024,256]{2,1,0:T(8,128)(2,1)S(1)}, bf16[1,1024,256]{2,1,0:T(8,128)(2,1)}, u32[]{:S(2)}) copy-start(bf16[1,1024,256]{2,1,0:T(8,128)(2,1)} %out_hbm.3) | copy-start | bytes 1572868
  8.6 37.2 %copy-start.8 = (bf16[2,128,256]{2,1,0:T(8,128)(2,1)S(1)}, bf16[2,128,256]{2,1,0:T(8,128)(2,1)}, u32[]{:S(2)}) copy-start(bf16[2,128,256]{2,1,0:T(8,128)(2,1)} %c_ref.1) | copy-start | bytes 393220
  8.6 37.2 %copy-start.9 = (bf16[2,128,256]{2,1,0:T(8,128)(2,1)S(1)}, bf16[2,128,256]{2,1,0:T(8,128)(2,1)}, u32[]{:S(2)}) copy-start(bf16[2,128,256]{2,1,0:T(8,128)(2,1)} %cot_ref.1) | copy-start | bytes 393220
  8.6 37.2 %copy-start.10 = (s32[2,128]{1,0:T(2,128)S(1)}, s32[2,128]{1,0:T(2,128)}, u32[]{:S(2)}) copy-start(s32[2,128]{1,0:T(2,128)} %seg_ref.1) | copy-start | bytes 3076
  45.8 30.6 %copy-start.3 = (bf16[4096,256]{1,0:T(8,128)(2,1)S(1)}, bf16[4096,256]{1,0:T(8,128)(2,1)}, u32[]{:S(2)}) copy-start(bf16[4096,256]{1,0:T(8,128)(2,1)} %basis_hbm.3) | copy-start | bytes 6291460
  45.8 30.6 %copy-start.5 = (bf16[1,1024,256]{2,1,0:T(8,128)(2,1)S(1)}, bf16[1,1024,256]{2,1,0:T(8,128)(2,1)}, u32[]{:S(2)}) copy-start(bf16[1,1024,256]{2,1,0:T(8,128)(2,1)} %out_hbm.3) | copy-start | bytes 1572868
  60.7 0.7 copy-start.6
  76.4 3.4 %copy-start.1 = (bf16[1,4096,1024]{2,1,0:T(8,128)(2,1)S(1)}, bf16[1,4096,1024]{2,1,0:T(8,128)(2,1)}, u32[]{:S(2)}) copy-start(bf16[1,4096,1024]{2,1,0:T(8,128)(2,1)} %value_hbm.3) | copy-start | bytes 25165828
  79.8 0.9 %copy-start.7 = (bf16[16,16,256]{2,1,0:T(8,128)(2,1)S(1)}, bf16[16,16,256]{2,1,0:T(8,128)(2,1)}, u32[]{:S(2)}) copy-start(bf16[16,16,256]{2,1,0:T(8,128)(2,1)} %shard_map.96.factor_ref) | copy-start | bytes 393220

commit v3 on v1

v3 whole, which is shorter than its diff:
```python
import jax
import jax.numpy as jnp
from jax import lax
from jax.experimental import pallas as pl
from jax.experimental.pallas import tpu as pltpu
from jax.sharding import PartitionSpec as P

EPS = 1e-05
MESH = pl.DeviceIdType.MESH
F32 = jnp.float32
BF16 = jnp.bfloat16
VMEM_LIMIT = 60 * 1024 * 1024


def mm(a, b, dims=((1,), (0,))):
    return lax.dot_general(a, b, (dims, ((), ())), preferred_element_type=F32)


def mixing_pair(seg_row):
    rows = seg_row.shape[1]
    across = jnp.broadcast_to(seg_row, (rows, rows))
    down = across.T
    i = lax.broadcasted_iota(jnp.int32, (rows, rows), 0)
    j = lax.broadcasted_iota(jnp.int32, (rows, rows), 1)
    same = across == down
    low = jnp.where(same & (j <= i), 1.0, 0.0).astype(F32)
    high = jnp.where(same & (i <= j), 1.0, 0.0).astype(F32)
    mixing = (low / jnp.sum(low, axis=1, keepdims=True)).astype(BF16)
    mixing_t = (high / jnp.sum(high, axis=0, keepdims=True)).astype(BF16)
    return mixing, mixing_t


class Place:
    def __init__(self):
        self.s = lax.axis_index("section")
        self.d = lax.axis_index("dp")
        self.z = self.s // 2
        self.xl = self.s % 2
        self.y = self.d // 4
        self.xh = (self.d // 2) % 2
        self.core = self.d % 2
        self.x = self.xh * 2 + self.xl

    def dp_peer(self, k):
        return (self.s, (self.d + k) % 16)

    def z_peer(self, k):
        return (((self.z + k) % 8) * 2 + self.xl, self.d)

    def y_peer(self, k):
        return (self.s, ((self.y + k) % 4) * 4 + self.xh * 2 + self.core)

    def x_peer(self, k):
        x = (self.x + k) % 4
        return (self.z * 2 + x % 2, self.y * 4 + (x // 2) * 2 + self.core)

    def core_peer(self):
        return (self.s, self.y * 4 + self.xh * 2 + (self.core + 1) % 2)


def piece_of(d):
    return (d % 2) * 8 + d // 2


def send(src, dst, send_sem, recv_sem, peer):
    copy = pltpu.make_async_remote_copy(
        src_ref=src, dst_ref=dst, send_sem=send_sem, recv_sem=recv_sem,
        device_id=peer, device_id_type=MESH,
    )
    copy.start()
    return copy


def far_first(at):
    hops = lambda o: min(o[0], 4 - o[0]) + 2 * o[1]
    offsets = [(y, xh, c) for y in range(4) for xh in range(2) for c in range(2) if (y, xh, c) != (0, 0, 0)]
    offsets.sort(key=lambda o: -hops(o))
    peers = []
    for y, xh, c in offsets:
        y_to, xh_to, c_to = (at.y + y) % 4, (at.xh + xh) % 2, (at.core + c) % 2
        peers.append(((at.s, y_to * 4 + xh_to * 2 + c_to), c_to * 8 + y_to * 2 + xh_to))
    return peers


def relay(
    basis_hbm, gain_ref, value_hbm, out_hbm, c_ref, cot_ref, seg_ref, gv_ref, go_ref, gg_ref,
    value, basis, out, scaled_t, step, gain_pad, every, xs, ps, es, hs, invs,
    part, part_b, slots, whole, go_wide,
    load_sem, z_send, z_recv, a_send, a_recv, b_send, b_recv, c_send, c_recv,
    rs_send, rs_recv, ag_send, ag_recv,
):
    at = Place()
    width = basis.shape[0]
    block = 512
    blocks = width // block
    loads = [
        pltpu.make_async_copy(basis_hbm, basis, load_sem.at[0]),
        pltpu.make_async_copy(out_hbm.at[0], out, load_sem.at[1]),
    ]
    for i in range(blocks):
        rows = pl.ds(i * block, block)
        loads.append(pltpu.make_async_copy(value_hbm.at[0, rows, :], value.at[rows, :], load_sem.at[2 + i]))
    for load in loads:
        load.start()
    barrier = pltpu.get_barrier_semaphore()
    peers = [at.z_peer(k) for k in (4, 3, 5, 2, 6, 1, 7)] + [at.dp_peer(k) for k in range(1, 16)]
    peers += [at.x_peer(1), at.x_peer(3)]
    for peer in peers:
        pl.semaphore_signal(barrier, inc=1, device_id=peer, device_id_type=MESH)

    gram = jnp.zeros((256, 256), F32)
    own_step = jnp.zeros((256, 256), F32)
    loads[0].wait()
    loads[1].wait()
    for i in range(blocks):
        lanes = slice(i * block, (i + 1) * block)
        chunk = basis[lanes, :]
        chunk_t = chunk.astype(F32).T
        gram = gram + mm(chunk_t.astype(BF16), chunk)
        scaled = (chunk_t * gain_ref[0:1, lanes]).astype(BF16)
        scaled_t[:, lanes] = scaled
        loads[2 + i].wait()
        through = mm(value[lanes, :], out[...]).astype(BF16)
        own_step = own_step + mm(scaled, through)
    step[...] = own_step.astype(BF16).reshape(16, 16, 256)
    own = every.at[at.core, at.z % 2, at.z // 2, at.y, at.xh, at.xl]
    own[...] = step[piece_of(at.d)]

    pl.semaphore_wait(barrier, len(peers))
    over_z = [send(own, own, z_send.at[k], z_recv.at[k], at.z_peer(k)) for k in (4, 3, 5, 2, 6, 1, 7)]

    gram_b = gram.astype(BF16)
    for i in range(16):
        gain_pad[i : i + 1, :] = gain_ref[0:1, i * 256 : (i + 1) * 256]
    gain_pad[16:128, :] = jnp.zeros((112, 256), F32)
    gain_cols = gain_pad[...].T
    lane = lax.broadcasted_iota(jnp.int32, gain_cols.shape, 1)
    own_gain = jnp.sum(jnp.where(lane == at.d, gain_cols, 0.0), axis=1, keepdims=True)
    cols = pl.ds(pl.multiple_of((at.d // 2) * 128, 128), 128)
    folded = mm(scaled_t[...], value[:, cols]).astype(BF16)
    micros = c_ref.shape[0]
    mixings = [mixing_pair(seg_ref[m : m + 1, :].astype(F32)) for m in range(micros)]
    cs = [c_ref[m].astype(F32) for m in range(micros)]
    hh = [mm(c_ref[m], gram_b) for m in range(micros)]

    for copy in over_z:
        copy.wait_recv()
    own0 = every.at[at.core, 0, :, at.y, at.xh, at.xl]
    own1 = every.at[at.core, 1, :, at.y, at.xh, at.xl]
    first = []
    for k in (2, 1, 3):
        first.append(send(own0, own0, a_send.at[0, k], a_recv.at[0, k], at.x_peer(k)))
        first.append(send(own1, own1, a_send.at[1, k], a_recv.at[1, k], at.y_peer(k)))
    for copy in first:
        copy.wait_recv()
    second = []
    for q in range(4):
        row0 = every.at[at.core, 0, q, at.y]
        row1 = every.at[at.core, 1, q, :, at.xh, at.xl]
        group = []
        for k in (2, 1, 3):
            group.append(send(row0, row0, b_send.at[0, q, k], b_recv.at[0, q, k], at.y_peer(k)))
            group.append(send(row1, row1, b_send.at[1, q, k], b_recv.at[1, q, k], at.x_peer(k)))
        second.append(group)
    across = []

    def land(q):
        for copy in second[q]:
            copy.wait_recv()
        half = every.at[at.core, :, q]
        across.append(send(half, half, c_send.at[q], c_recv.at[q], at.core_peer()))

    def step_of(s):
        z, xl = s // 2, s % 2
        return every[:, z % 2, z // 2, :, :, xl].reshape(256, 256)

    def forward(s):
        n = step_of(s)
        ng = mm(n, gram_b).astype(BF16)
        for m in range(micros):
            cb = cs[m].astype(BF16)
            ms = jnp.sum(cs[m] * hh[m], axis=1, keepdims=True) * (1.0 / width)
            inv = lax.rsqrt(jnp.maximum(ms, 0.0) + EPS)
            e = mm(cb, n)
            xs[s, m] = (inv * cs[m]).astype(BF16)
            es[s, m] = e
            hs[s, m] = hh[m]
            invs[s, m] = jnp.broadcast_to(inv, invs.shape[2:])
            if s < 15:
                f = mm(cb, ng)
                cs[m] = cs[m] + mm(mixings[m][0], (inv * e).astype(BF16))
                hh[m] = hh[m] + mm(mixings[m][0], (inv * f).astype(BF16))

    land(0)
    across[0].wait_recv()
    for q in range(4):
        forward(4 * q)
        forward(4 * q + 1)
        if q < 3:
            land(q + 1)
        forward(4 * q + 2)
        forward(4 * q + 3)
        if q < 3:
            across[q + 1].wait_recv()

    gs = [cot_ref[m].astype(F32) for m in range(micros)]
    for s in reversed(range(16)):
        n = step_of(s)
        for m in range(micros):
            p = mm(mixings[m][1], gs[m].astype(BF16))
            pb = p.astype(BF16)
            ps[s, m] = pb
            if s > 0:
                q = mm(pb, n, ((1,), (1,)))
                inv = invs[s, m][:, :1]
                t = jnp.sum(p * es[s, m], axis=1, keepdims=True)
                gs[m] = gs[m] + inv * q - (inv * inv * inv * t * (1.0 / width)) * hs[s, m]

    total = mm(xs[at.s, 0], ps[at.s, 0], ((0,), (0,)))
    for m in range(1, micros):
        total = total + mm(xs[at.s, m], ps[at.s, m], ((0,), (0,)))
    part[...] = total.reshape(16, 16, 256)
    part_b[...] = total.astype(BF16).reshape(16, 16, 256)
    others = far_first(at)
    pieces = [
        send(part_b.at[piece], slots.at[i], rs_send.at[i], rs_recv.at[i], peer)
        for i, (peer, piece) in enumerate(others)
    ]
    mine = part[piece_of(at.d)]
    for i in reversed(range(15)):
        pieces[i].wait_recv()
        mine = mine + slots[i].astype(F32)
    summed = whole.at[piece_of(at.d)]
    summed[...] = mine.astype(BF16)
    spread = [
        send(summed, summed, ag_send.at[i], ag_recv.at[i], peer) for i, (peer, piece) in enumerate(others)
    ]
    for copy in spread:
        copy.wait_recv()

    factor = whole[...].reshape(256, 256)
    own_rows = pl.ds(pl.multiple_of(at.d * 256, 256), 256)
    left = mm(basis[own_rows, :], factor).astype(BF16)
    plain = mm(left, out[...], ((1,), (1,)))
    gv_ref[0] = own_gain * plain
    go_wide[...] = mm(folded, factor, ((0,), (0,)))
    go_ref[0] = go_wide[pl.ds(pl.multiple_of((at.d % 2) * 64, 64), 64), :]
    sums = jnp.sum(plain * value[own_rows, :].astype(F32), axis=1, keepdims=True)
    gg_ref[...] = jnp.broadcast_to(sums, (256, 128)).T[0:1, :]
    for copy in over_z + first + sum(second, []) + across + pieces + spread:
        copy.wait_send()


def shards(coeffs, cotangent, segment_ids, basis_matrix, section_gains, value_weight, out_weight):
    vmem = pl.BlockSpec(memory_space=pltpu.VMEM)
    anywhere = pl.BlockSpec(memory_space=pl.ANY)
    dma = pltpu.SemaphoreType.DMA
    return pl.pallas_call(
        relay,
        out_shape=(
            jax.ShapeDtypeStruct((1, 256, 1024), F32),
            jax.ShapeDtypeStruct((1, 64, 256), F32),
            jax.ShapeDtypeStruct((1, 256), F32),
        ),
        in_specs=[anywhere, vmem, anywhere, anywhere, vmem, vmem, vmem],
        out_specs=(vmem, vmem, vmem),
        scratch_shapes=[
            pltpu.VMEM((4096, 1024), BF16),
            pltpu.VMEM((4096, 256), BF16),
            pltpu.VMEM((1024, 256), BF16),
            pltpu.VMEM((256, 4096), BF16),
            pltpu.VMEM((16, 16, 256), BF16),
            pltpu.VMEM((128, 256), F32),
            pltpu.VMEM((2, 2, 4, 4, 2, 2, 16, 256), BF16),
            pltpu.VMEM((16, 2, 128, 256), BF16),
            pltpu.VMEM((16, 2, 128, 256), BF16),
            pltpu.VMEM((16, 2, 128, 256), F32),
            pltpu.VMEM((16, 2, 128, 256), F32),
            pltpu.VMEM((16, 2, 128, 128), F32),
            pltpu.VMEM((16, 16, 256), F32),
            pltpu.VMEM((16, 16, 256), BF16),
            pltpu.VMEM((15, 16, 256), BF16),
            pltpu.VMEM((16, 16, 256), BF16),
            pltpu.VMEM((128, 256), F32),
            dma((10,)), dma((8,)), dma((8,)), dma((2, 4)), dma((2, 4)),
            dma((2, 4, 4)), dma((2, 4, 4)), dma((4,)), dma((4,)),
            dma((15,)), dma((15,)), dma((15,)), dma((15,)),
        ],
        compiler_params=pltpu.CompilerParams(
            collective_id=0, has_side_effects=True, vmem_limit_bytes=VMEM_LIMIT
        ),
    )(basis_matrix, section_gains, value_weight, out_weight, coeffs, cotangent, segment_ids)


def solution(mesh):
    placed = (
        P(None, "dp", None),
        P(None, "dp", None),
        P(None, "dp"),
        P(),
        P("section", None),
        P("section", None, None),
        P("section", None, None),
    )
    return jax.shard_map(
        shards,
        mesh=mesh,
        in_specs=placed,
        out_specs=(P("section", "dp", None), P("section", "dp", None), P("section", "dp")),
        check_vma=False,
    )
```

time: 261 us -> 66.9 us (0.26)
  waiting for transfers between devices: 215 us -> 0 us
  Pallas kernels: 14.7 us -> 61 us
  between operations: 14.1 us -> 0.64 us
  matrix products: 13.4 us -> 0 us
    psum x1 -> x0, waiting for transfers between devices: 148 us -> none  [shards(): factor = lax.psum(factor_part.astype(BF16), 'dp')]
    all_gather x1 -> x0, waiting for transfers between devices: 66.8 us -> none  [shards(): steps = lax.all_gather(step, 'section')]
    pallas_call x1, Pallas kernels: 14.7 us -> 61 us  [shards(): pl.pallas_call(relay, out_shape=(jax.ShapeDtypeStruct((1, 256, 1024), F32...]
    dot_general x5 -> x0, matrix products: 13.4 us -> none  [mm(): return lax.dot_general(a, b, (dims, ((), ())), preferred_element_type=F32)]
  transfers between devices with their start and end apart: 2 -> 0, of which waited for: 2 -> 0; matrix products, arithmetic and copies ran while one was open for 1% -> 0% of each run, Pallas kernels for 0% -> 0%
where the time goes in v3:
time: 66.9 us; the launch traced here: 66.7 us
  Pallas kernels  61 us (91%)
  local copies, waits for them, and re-layouts  5.01 us (7%)
    pallas_call x1, Pallas kernels, shards(): pl.pallas_call(relay, out_shape=(jax.ShapeDtypeStruct((1, 256, 1024), F32...  61 us
    unnamed x3, local copies, waits for them, and re-layouts  5.01 us

profile of v3, /device:TPU:1, one launch (start us, length us, event | category | flops | bytes accessed | tf_op | source)
XLA Modules:
  0.0 66.7 jit_solution(12364854654929026342)
XLA Ops:
  0.6 61.0 %shard_map.94 = (f32[1,256,1024]{2,1,0:T(8,128)}, f32[1,64,256]{2,1,0:T(8,128)}, f32[1,256]{1,0:T(1,128)}) custom-call(bf16[4096,256]{1,0:T(8,128)(2,1)} %basis_hbm.1, f32[1,4096]{1,0:T(1,128)} %gain_ref.1, bf16[1,4096,1024]{2,1,0:T(8,128)(2,1)} %value_hbm.1, bf16[1,1024,256]{2,1,0:T(8,128)(2,1)} %out_hbm.1, bf16[2,128,256]{2,1,0:T(8,128)(2,1)} %c_ref.1, ...), custom_call_target="tpu_custom_call" | custom-call | tf_op jit(solution)/shard_map/pallas_call | solution.py:258
  61.7 2.3 %copy.13 = f32[1,256,1024]{2,1,0:T(8,128)} copy(f32[1,256,1024]{2,1,0:T(8,128)} %get-tuple-element.6) | data formatting | bytes 2097152
  64.0 1.5 %copy.14 = f32[1,64,256]{2,1,0:T(8,128)} copy(f32[1,64,256]{2,1,0:T(8,128)} %get-tuple-element.7) | data formatting | bytes 131072
  65.4 1.2 %copy.15 = f32[1,256]{1,0:T(1,128)} copy(f32[1,256]{1,0:T(1,128)} %get-tuple-element.8) | data formatting | bytes 2048

commit v4 on v3

v4 whole, which is shorter than its diff:
```python
import jax
import jax.numpy as jnp
from jax import lax
from jax.experimental import pallas as pl
from jax.experimental.pallas import tpu as pltpu
from jax.sharding import PartitionSpec as P

EPS = 1e-05
MESH = pl.DeviceIdType.MESH
F32 = jnp.float32
BF16 = jnp.bfloat16
VMEM_LIMIT = 58 * 1024 * 1024


def mm(a, b, dims=((1,), (0,))):
    return lax.dot_general(a, b, (dims, ((), ())), preferred_element_type=F32)


def mixing_pair(seg_row):
    rows = seg_row.shape[1]
    across = jnp.broadcast_to(seg_row, (rows, rows))
    down = across.T
    i = lax.broadcasted_iota(jnp.int32, (rows, rows), 0)
    j = lax.broadcasted_iota(jnp.int32, (rows, rows), 1)
    same = across == down
    low = jnp.where(same & (j <= i), 1.0, 0.0).astype(F32)
    high = jnp.where(same & (i <= j), 1.0, 0.0).astype(F32)
    mixing = (low / jnp.sum(low, axis=1, keepdims=True)).astype(BF16)
    mixing_t = (high / jnp.sum(high, axis=0, keepdims=True)).astype(BF16)
    return mixing, mixing_t


class Place:
    def __init__(self):
        self.s = lax.axis_index("section")
        self.d = lax.axis_index("dp")
        self.z = self.s // 2
        self.xl = self.s % 2
        self.y = self.d // 4
        self.xh = (self.d // 2) % 2
        self.core = self.d % 2
        self.x = self.xh * 2 + self.xl

    def dp_peer(self, k):
        return (self.s, (self.d + k) % 16)

    def z_peer(self, k):
        return (((self.z + k) % 8) * 2 + self.xl, self.d)

    def y_peer(self, k):
        return (self.s, ((self.y + k) % 4) * 4 + self.xh * 2 + self.core)

    def x_peer(self, k):
        x = (self.x + k) % 4
        return (self.z * 2 + x % 2, self.y * 4 + (x // 2) * 2 + self.core)

    def core_peer(self):
        return (self.s, self.y * 4 + self.xh * 2 + (self.core + 1) % 2)


def piece_of(d):
    return (d % 2) * 8 + d // 2


def send(src, dst, send_sem, recv_sem, peer):
    copy = pltpu.make_async_remote_copy(
        src_ref=src, dst_ref=dst, send_sem=send_sem, recv_sem=recv_sem,
        device_id=peer, device_id_type=MESH,
    )
    copy.start()
    return copy


def far_first(at):
    hops = lambda o: min(o[0], 4 - o[0]) + 2 * o[1]
    offsets = [(y, xh, c) for y in range(4) for xh in range(2) for c in range(2) if (y, xh, c) != (0, 0, 0)]
    offsets.sort(key=lambda o: -hops(o))
    peers = []
    for y, xh, c in offsets:
        y_to, xh_to, c_to = (at.y + y) % 4, (at.xh + xh) % 2, (at.core + c) % 2
        peers.append(((at.s, y_to * 4 + xh_to * 2 + c_to), c_to * 8 + y_to * 2 + xh_to))
    return peers


def relay(
    basis_hbm, gain_hbm, value_hbm, out_hbm, c_hbm, cot_hbm, seg_hbm,
    whole, folded_ref, own_gain_ref,
    out, value, value_cols, basis_half, basis, gain_half, gain, c_ref, cot_ref, seg_ref,
    part_n, part_nb, slot_n, gain_pad, every, xs, ps, es, hs, invs, part, part_b, slots,
    load_sem, n_send, n_recv, z_send, z_recv, y_send, y_recv, x_send, x_recv, c_send, c_recv,
    rs_send, rs_recv, ag_send, ag_recv,
):
    at = Place()
    width = basis.shape[0]
    half = width // 2
    cuts = (0, 512, 1024, 2048)
    start = pl.multiple_of(at.core * half, half)

    def load(i, src, dst):
        copy = pltpu.make_async_copy(src, dst, load_sem.at[i])
        copy.start()
        return copy

    early = [
        load(0, gain_hbm.at[:, pl.ds(start, half)], gain_half),
        load(1, basis_hbm.at[pl.ds(start, half), :], basis_half),
        load(2, out_hbm.at[0], out),
    ]
    for i in range(3):
        size = cuts[i + 1] - cuts[i]
        rows = pl.ds(pl.multiple_of(start + cuts[i], 512), size)
        early.append(load(3 + i, value_hbm.at[0, rows, :], value.at[pl.ds(cuts[i], size), :]))
    barrier = pltpu.get_barrier_semaphore()
    peers = [at.z_peer(k) for k in (4, 3, 5, 2, 6, 1, 7)] + [at.dp_peer(k) for k in range(1, 16)]
    peers += [at.x_peer(1), at.x_peer(3)]
    for peer in peers:
        pl.semaphore_signal(barrier, inc=1, device_id=peer, device_id_type=MESH)
    cols = pl.ds(pl.multiple_of((at.d // 2) * 128, 128), 128)
    late = [
        load(6, basis_hbm, basis),
        load(7, value_hbm.at[0, :, cols], value_cols),
        load(8, gain_hbm, gain),
        load(9, c_hbm, c_ref),
        load(10, seg_hbm, seg_ref),
        load(11, cot_hbm, cot_ref),
    ]

    partial = jnp.zeros((256, 256), F32)
    for copy in early[:3]:
        copy.wait()
    for i in range(3):
        lanes = slice(cuts[i], cuts[i + 1])
        scaled = (basis_half[lanes, :].astype(F32).T * gain_half[0:1, lanes]).astype(BF16)
        early[3 + i].wait()
        through = mm(value[lanes, :], out[...]).astype(BF16)
        partial = partial + mm(scaled, through)
    part_n[...] = partial.reshape(8, 32, 256)
    part_nb[...] = partial.astype(BF16).reshape(8, 32, 256)

    pl.semaphore_wait(barrier, len(peers))
    other = (at.core + 1) % 2
    swap = send(part_nb.at[other * 4 + at.y], slot_n, n_send, n_recv, at.core_peer())
    swap.wait_recv()
    own = every.at[at.core, at.z // 2, at.xl, at.z % 2, at.y]
    own[...] = (part_n[at.core * 4 + at.y] + slot_n[...].astype(F32)).astype(BF16)
    over_z = [send(own, own, z_send.at[k], z_recv.at[k], at.z_peer(k)) for k in (4, 3, 5, 2, 6, 1, 7)]

    for copy in late:
        copy.wait()
    gram = jnp.zeros((256, 256), F32)
    folded = jnp.zeros((256, 128), F32)
    for i in range(8):
        lanes = slice(i * 512, (i + 1) * 512)
        chunk = basis[lanes, :]
        chunk_t = chunk.astype(F32).T
        gram = gram + mm(chunk_t.astype(BF16), chunk)
        scaled = (chunk_t * gain[0:1, lanes]).astype(BF16)
        folded = folded + mm(scaled, value_cols[lanes, :])
    folded_ref[...] = folded.astype(BF16)
    gram_b = gram.astype(BF16)
    for i in range(16):
        gain_pad[i : i + 1, :] = gain[0:1, i * 256 : (i + 1) * 256]
    gain_pad[16:128, :] = jnp.zeros((112, 256), F32)
    gain_cols = gain_pad[...].T
    lane = lax.broadcasted_iota(jnp.int32, gain_cols.shape, 1)
    own_gain = jnp.sum(jnp.where(lane == at.d, gain_cols, 0.0), axis=1, keepdims=True)
    own_gain_ref[...] = jnp.broadcast_to(own_gain, own_gain_ref.shape)
    micros = c_ref.shape[0]
    mixings = [mixing_pair(seg_ref[m : m + 1, :].astype(F32)) for m in range(micros)]
    cs = [c_ref[m].astype(F32) for m in range(micros)]
    hh = [mm(c_ref[m], gram_b) for m in range(micros)]

    for copy in over_z:
        copy.wait_recv()
    over_y = []
    for q in range(4):
        mine = every.at[at.core, q, at.xl, :, at.y]
        over_y.append(
            [send(mine, mine, y_send.at[q, k], y_recv.at[q, k], at.y_peer(k)) for k in (2, 1, 3)]
        )
    over_x, across = [], []

    def pass_x(q):
        for copy in over_y[q]:
            copy.wait_recv()
        low = every.at[at.core, q, at.xl, :, pl.ds(0, 2)]
        high = every.at[at.core, q, at.xl, :, pl.ds(2, 2)]
        over_x.append([
            send(low, low, x_send.at[q, 0], x_recv.at[q, 0], at.x_peer(1)),
            send(high, high, x_send.at[q, 1], x_recv.at[q, 1], at.x_peer(3)),
        ])

    def pass_core(q):
        for copy in over_x[q]:
            copy.wait_recv()
        chunk = every.at[at.core, q]
        across.append(send(chunk, chunk, c_send.at[q], c_recv.at[q], at.core_peer()))

    def step_of(s):
        z, xl = s // 2, s % 2
        return every[:, z // 2, xl, z % 2].reshape(256, 256)

    def onward(s):
        return mm(step_of(s), gram_b).astype(BF16)

    def forward(s, ng):
        n = step_of(s)
        both = range(micros)
        es_ = [mm(cs[m].astype(BF16), n) for m in both]
        invs_ = []
        for m in both:
            ms = jnp.sum(cs[m] * hh[m], axis=1, keepdims=True) * (1.0 / width)
            invs_.append(lax.rsqrt(jnp.maximum(ms, 0.0) + EPS))
        fs_ = [mm(cs[m].astype(BF16), ng) for m in both] if s < 15 else []
        old = list(cs)
        for m in both:
            xs[s, m] = (invs_[m] * old[m]).astype(BF16)
            es[s, m] = es_[m]
            hs[s, m] = hh[m]
            invs[s, m] = jnp.broadcast_to(invs_[m], invs.shape[2:])
        if s == 15:
            return None
        ys_ = [mm(mixings[m][0], (invs_[m] * es_[m]).astype(BF16)) for m in both]
        for m in both:
            cs[m] = cs[m] + ys_[m]
        ng = onward(s + 1)
        zs_ = [mm(mixings[m][0], (invs_[m] * fs_[m]).astype(BF16)) for m in both]
        for m in both:
            hh[m] = hh[m] + zs_[m]
        return ng

    pass_x(0)
    pass_x(1)
    pass_core(0)
    pass_x(2)
    pass_core(1)
    across[0].wait_recv()
    ng = onward(0)
    ng = forward(0, ng)
    ng = forward(1, ng)
    pass_x(3)
    ng = forward(2, ng)
    pass_core(2)
    across[1].wait_recv()
    for s in (3, 4, 5):
        ng = forward(s, ng)
    pass_core(3)
    ng = forward(6, ng)
    across[2].wait_recv()
    for s in (7, 8, 9, 10):
        ng = forward(s, ng)
    across[3].wait_recv()
    for s in (11, 12, 13, 14, 15):
        ng = forward(s, ng)

    gs = [cot_ref[m].astype(F32) for m in range(micros)]
    for s in reversed(range(16)):
        n = step_of(s)
        both = range(micros)
        ps_ = [mm(mixings[m][1], gs[m].astype(BF16)) for m in both]
        pb_ = [p.astype(BF16) for p in ps_]
        qs_ = [mm(p, n, ((1,), (1,))) for p in pb_] if s > 0 else []
        for m in both:
            ps[s, m] = pb_[m]
            if s > 0:
                inv = invs[s, m][:, :1]
                t = jnp.sum(ps_[m] * es[s, m], axis=1, keepdims=True)
                gs[m] = (gs[m] - (inv * inv * inv * t * (1.0 / width)) * hs[s, m]) + inv * qs_[m]

    rows = micros * xs.shape[2]
    total = mm(xs[at.s].reshape(rows, 256), ps[at.s].reshape(rows, 256), ((0,), (0,)))
    part[...] = total.reshape(16, 16, 256)
    part_b[...] = total.astype(BF16).reshape(16, 16, 256)
    others = far_first(at)
    pieces = [
        send(part_b.at[piece], slots.at[i], rs_send.at[i], rs_recv.at[i], peer)
        for i, (peer, piece) in enumerate(others)
    ]
    mine = part[piece_of(at.d)]
    for i in reversed(range(15)):
        pieces[i].wait_recv()
        mine = mine + slots[i].astype(F32)
    summed = whole.at[piece_of(at.d)]
    summed[...] = mine.astype(BF16)
    spread = [
        send(summed, summed, ag_send.at[i], ag_recv.at[i], peer) for i, (peer, piece) in enumerate(others)
    ]
    for copy in [swap] + over_z + sum(over_y, []) + sum(over_x, []) + across + pieces:
        copy.wait_send()
    for copy in spread:
        copy.wait()


def finish(factor_hbm, folded_hbm, own_gain_hbm, out_hbm, basis_hbm, value_hbm, gv_hbm, go_hbm, gg_hbm,
           factor_ref, folded, own_gain, out, basis, value, gv, go, gg, load_sem, store_sem):
    d = lax.axis_index("dp")
    rows = pl.ds(pl.multiple_of(d * 256, 256), 256)
    loads = [
        pltpu.make_async_copy(factor_hbm, factor_ref, load_sem.at[0]),
        pltpu.make_async_copy(basis_hbm.at[rows, :], basis, load_sem.at[1]),
        pltpu.make_async_copy(out_hbm.at[0], out, load_sem.at[2]),
        pltpu.make_async_copy(own_gain_hbm, own_gain, load_sem.at[3]),
        pltpu.make_async_copy(value_hbm.at[0, rows, :], value, load_sem.at[4]),
        pltpu.make_async_copy(folded_hbm, folded, load_sem.at[5]),
    ]
    for load in loads:
        load.start()
    for load in loads:
        load.wait()
    factor = factor_ref[...].reshape(256, 256)
    left = mm(basis[...], factor).astype(BF16)
    gain = own_gain[:, :1]
    sums = jnp.zeros((256, 1), F32)
    stores = []
    for i in range(4):
        lanes = slice(i * 256, (i + 1) * 256)
        plain = mm(left, out[lanes, :], ((1,), (1,)))
        gv[:, lanes] = gain * plain
        stores.append(pltpu.make_async_copy(
            gv.at[:, lanes], gv_hbm.at[0, :, lanes], store_sem.at[i]))
        stores[-1].start()
        sums = sums + jnp.sum(plain * value[:, lanes].astype(F32), axis=1, keepdims=True)
    go[...] = mm(folded[...], factor, ((0,), (0,)))
    own = pl.ds(pl.multiple_of((d % 2) * 64, 64), 64)
    stores.append(pltpu.make_async_copy(go.at[own, :], go_hbm.at[0], store_sem.at[4]))
    stores[-1].start()
    gg[...] = jnp.broadcast_to(sums, (256, 128)).T[0:1, :]
    stores.append(pltpu.make_async_copy(gg, gg_hbm, store_sem.at[5]))
    stores[-1].start()
    for store in stores:
        store.wait()


def shards(coeffs, cotangent, segment_ids, basis_matrix, section_gains, value_weight, out_weight):
    vmem = pl.BlockSpec(memory_space=pltpu.VMEM)
    hbm = pl.BlockSpec(memory_space=pltpu.HBM)
    dma = pltpu.SemaphoreType.DMA
    shape = jax.ShapeDtypeStruct
    handed = pl.pallas_call(
        relay,
        out_shape=(
            shape((16, 16, 256), BF16),
            shape((256, 128), BF16),
            shape((256, 128), F32),
        ),
        in_specs=[hbm] * 7,
        out_specs=(vmem,) * 3,
        scratch_shapes=[
            pltpu.VMEM((1024, 256), BF16),
            pltpu.VMEM((2048, 1024), BF16),
            pltpu.VMEM((4096, 128), BF16),
            pltpu.VMEM((2048, 256), BF16),
            pltpu.VMEM((4096, 256), BF16),
            pltpu.VMEM((1, 2048), F32),
            pltpu.VMEM((1, 4096), F32),
            pltpu.VMEM((2, 128, 256), BF16),
            pltpu.VMEM((2, 128, 256), BF16),
            pltpu.VMEM((2, 128), jnp.int32),
            pltpu.VMEM((8, 32, 256), F32),
            pltpu.VMEM((8, 32, 256), BF16),
            pltpu.VMEM((32, 256), BF16),
            pltpu.VMEM((128, 256), F32),
            pltpu.VMEM((2, 4, 2, 2, 4, 32, 256), BF16),
            pltpu.VMEM((16, 2, 128, 256), BF16),
            pltpu.VMEM((16, 2, 128, 256), BF16),
            pltpu.VMEM((16, 2, 128, 256), F32),
            pltpu.VMEM((16, 2, 128, 256), F32),
            pltpu.VMEM((16, 2, 128, 128), F32),
            pltpu.VMEM((16, 16, 256), F32),
            pltpu.VMEM((16, 16, 256), BF16),
            pltpu.VMEM((15, 16, 256), BF16),
            dma((12,)), dma, dma, dma((8,)), dma((8,)),
            dma((4, 4)), dma((4, 4)), dma((4, 2)), dma((4, 2)), dma((4,)), dma((4,)),
            dma((15,)), dma((15,)), dma((15,)), dma((15,)),
        ],
        compiler_params=pltpu.CompilerParams(
            collective_id=0, has_side_effects=True, vmem_limit_bytes=VMEM_LIMIT
        ),
    )(basis_matrix, section_gains, value_weight, out_weight, coeffs, cotangent, segment_ids)
    return pl.pallas_call(
        finish,
        out_shape=(
            shape((1, 256, 1024), F32),
            shape((1, 64, 256), F32),
            shape((1, 256), F32),
        ),
        in_specs=[hbm] * 6,
        out_specs=(hbm,) * 3,
        scratch_shapes=[
            pltpu.VMEM((16, 16, 256), BF16),
            pltpu.VMEM((256, 128), BF16),
            pltpu.VMEM((256, 128), F32),
            pltpu.VMEM((1024, 256), BF16),
            pltpu.VMEM((256, 256), BF16),
            pltpu.VMEM((256, 1024), BF16),
            pltpu.VMEM((256, 1024), F32),
            pltpu.VMEM((128, 256), F32),
            pltpu.VMEM((1, 256), F32),
            dma((6,)),
            dma((6,)),
        ],
        compiler_params=pltpu.CompilerParams(vmem_limit_bytes=VMEM_LIMIT),
    )(*handed, out_weight, basis_matrix, value_weight)


def solution(mesh):
    placed = (
        P(None, "dp", None),
        P(None, "dp", None),
        P(None, "dp"),
        P(),
        P("section", None),
        P("section", None, None),
        P("section", None, None),
    )
    return jax.shard_map(
        shards,
        mesh=mesh,
        in_specs=placed,
        out_specs=(P("section", "dp", None), P("section", "dp", None), P("section", "dp")),
        check_vma=False,
    )
```

time: 66.9 us -> 57.3 us (0.86)
  local copies, waits for them, and re-layouts: 5.01 us -> 0 us
  Pallas kernels: 61 us -> 56.6 us
    unnamed x3 -> x0, local copies, waits for them, and re-layouts: 5.01 us -> none
    pallas_call x1 -> x2, Pallas kernels: 61 us -> 56.6 us  [the longest x1 53.8 us: shards(): pl.pallas_call(relay, out_shape=(shape((16, 16, 256), BF16), shape((256,...]
where the time goes in v4:
time: 57.3 us; the launch traced here: 57.2 us
  Pallas kernels  56.6 us (99%)
  between operations  0.64 us (1%)
    pallas_call x1, Pallas kernels, shards(): pl.pallas_call(relay, out_shape=(shape((16, 16, 256), BF16), shape((256,...  53.8 us
    pallas_call x1, Pallas kernels, shards(): pl.pallas_call(finish, out_shape=(shape((1, 256, 1024), F32), shape((1, 6...  2.82 us

profile of v4, /device:TPU:1, one launch (start us, length us, event | category | flops | bytes accessed | tf_op | source)
XLA Modules:
  0.0 57.2 jit_solution(13839839142605993480)
XLA Ops:
  0.6 53.8 %shard_map.94 = (bf16[16,16,256]{2,1,0:T(8,128)(2,1)}, bf16[256,128]{1,0:T(8,128)(2,1)}, f32[256,128]{1,0:T(8,128)}) custom-call(bf16[4096,256]{1,0:T(8,128)(2,1)} %basis_hbm.3, f32[1,4096]{1,0:T(1,128)} %gain_hbm.1, bf16[1,4096,1024]{2,1,0:T(8,128)(2,1)} %value_hbm.3, bf16[1,1024,256]{2,1,0:T(8,128)(2,1)} %out_hbm.3, bf16[2,128,256]{2,1,0:T(8,128)(2,1)} %c_hbm.1, ...), custom_call_target="tpu_custom_call" | custom-call | tf_op jit(solution)/shard_map/pallas_call | solution.py:339
  54.4 2.8 %shard_map.95 = (f32[1,256,1024]{2,1,0:T(8,128)}, f32[1,64,256]{2,1,0:T(8,128)}, f32[1,256]{1,0:T(1,128)}) custom-call(bf16[16,16,256]{2,1,0:T(8,128)(2,1)} %get-tuple-element.6.factor_hbm, bf16[256,128]{1,0:T(8,128)(2,1)} %get-tuple-element.7.folded_hbm, f32[256,128]{1,0:T(8,128)} %get-tuple-element.8.own_gain_hbm, bf16[1,1024,256]{2,1,0:T(8,128)(2,1)} %out_hbm.3, ...), custom_call_target="tpu_custom_call" | custom-call | tf_op jit(solution)/shard_map/pallas_call | solution.py:380

commit v5 on v4

--- a/solution.py
+++ b/solution.py
@@ -141,9 +141,9 @@
     other = (at.core + 1) % 2
     swap = send(part_nb.at[other * 4 + at.y], slot_n, n_send, n_recv, at.core_peer())
     swap.wait_recv()
-    own = every.at[at.core, at.z // 2, at.xl, at.z % 2, at.y]
+    own = every.at[at.core, at.z, at.xl, at.y]
     own[...] = (part_n[at.core * 4 + at.y] + slot_n[...].astype(F32)).astype(BF16)
-    over_z = [send(own, own, z_send.at[k], z_recv.at[k], at.z_peer(k)) for k in (4, 3, 5, 2, 6, 1, 7)]
+    over_z = [send(own, own, z_send.at[k], z_recv.at[at.z], at.z_peer(k)) for k in (4, 3, 5, 2, 6, 1, 7)]
 
     for copy in late:
         copy.wait()
@@ -170,35 +170,52 @@
     cs = [c_ref[m].astype(F32) for m in range(micros)]
     hh = [mm(c_ref[m], gram_b) for m in range(micros)]
 
-    for copy in over_z:
-        copy.wait_recv()
-    over_y = []
-    for q in range(4):
-        mine = every.at[at.core, q, at.xl, :, at.y]
+    bounds = (0, 1, 2, 4, 6, 8)
+    over_y, over_x, across = [], [], []
+
+    def arrived(z):
+        @pl.when(at.z != z)
+        def _():
+            there = every.at[at.core, z, at.xl, at.y]
+            pltpu.make_async_remote_copy(
+                src_ref=there, dst_ref=there, send_sem=z_send.at[0], recv_sem=z_recv.at[z],
+                device_id=at.core_peer(), device_id_type=MESH,
+            ).wait_recv()
+
+    def planes(q):
+        return pl.ds(bounds[q], bounds[q + 1] - bounds[q])
+
+    def start_y(q):
+        for z in range(bounds[q], bounds[q + 1]):
+            arrived(z)
+        mine = every.at[at.core, planes(q), at.xl, at.y]
         over_y.append(
             [send(mine, mine, y_send.at[q, k], y_recv.at[q, k], at.y_peer(k)) for k in (2, 1, 3)]
         )
-    over_x, across = [], []
-
-    def pass_x(q):
+
+    def start_x(q):
         for copy in over_y[q]:
             copy.wait_recv()
-        low = every.at[at.core, q, at.xl, :, pl.ds(0, 2)]
-        high = every.at[at.core, q, at.xl, :, pl.ds(2, 2)]
+        low = every.at[at.core, planes(q), at.xl, pl.ds(0, 2)]
+        high = every.at[at.core, planes(q), at.xl, pl.ds(2, 2)]
         over_x.append([
             send(low, low, x_send.at[q, 0], x_recv.at[q, 0], at.x_peer(1)),
             send(high, high, x_send.at[q, 1], x_recv.at[q, 1], at.x_peer(3)),
         ])
 
-    def pass_core(q):
+    def start_core(q):
         for copy in over_x[q]:
             copy.wait_recv()
-        chunk = every.at[at.core, q]
+        chunk = every.at[at.core, planes(q)]
         across.append(send(chunk, chunk, c_send.at[q], c_recv.at[q], at.core_peer()))
+
+    def sent(copies):
+        for copy in copies:
+            copy.wait_send()
 
     def step_of(s):
         z, xl = s // 2, s % 2
-        return every[:, z // 2, xl, z % 2].reshape(256, 256)
+        return every[:, z, xl].reshape(256, 256)
 
     def onward(s):
         return mm(step_of(s), gram_b).astype(BF16)
@@ -229,27 +246,36 @@
             hh[m] = hh[m] + zs_[m]
         return ng
 
-    pass_x(0)
-    pass_x(1)
-    pass_core(0)
-    pass_x(2)
-    pass_core(1)
+    start_y(0)
+    start_y(1)
+    sent(over_y[0])
+    start_y(2)
+    start_x(0)
+    sent(over_y[1])
+    start_y(3)
+    start_x(1)
+    sent(over_y[2])
+    start_y(4)
+    start_core(0)
+    start_x(2)
+    start_core(1)
+    start_x(3)
     across[0].wait_recv()
+    across[1].wait_recv()
     ng = onward(0)
-    ng = forward(0, ng)
-    ng = forward(1, ng)
-    pass_x(3)
-    ng = forward(2, ng)
-    pass_core(2)
-    across[1].wait_recv()
-    for s in (3, 4, 5):
+    for s in (0, 1, 2):
         ng = forward(s, ng)
-    pass_core(3)
-    ng = forward(6, ng)
+    start_core(2)
+    start_x(4)
+    start_core(3)
     across[2].wait_recv()
+    for s in (3, 4, 5, 6):
+        ng = forward(s, ng)
+    start_core(4)
+    across[3].wait_recv()
     for s in (7, 8, 9, 10):
         ng = forward(s, ng)
-    across[3].wait_recv()
+    across[4].wait_recv()
     for s in (11, 12, 13, 14, 15):
         ng = forward(s, ng)
 
@@ -285,8 +311,7 @@
     spread = [
         send(summed, summed, ag_send.at[i], ag_recv.at[i], peer) for i, (peer, piece) in enumerate(others)
     ]
-    for copy in [swap] + over_z + sum(over_y, []) + sum(over_x, []) + across + pieces:
-        copy.wait_send()
+    sent([swap] + over_z + sum(over_y[3:], []) + sum(over_x, []) + across + pieces)
     for copy in spread:
         copy.wait()
 
@@ -360,7 +385,7 @@
             pltpu.VMEM((8, 32, 256), BF16),
             pltpu.VMEM((32, 256), BF16),
             pltpu.VMEM((128, 256), F32),
-            pltpu.VMEM((2, 4, 2, 2, 4, 32, 256), BF16),
+            pltpu.VMEM((2, 8, 2, 4, 32, 256), BF16),
             pltpu.VMEM((16, 2, 128, 256), BF16),
             pltpu.VMEM((16, 2, 128, 256), BF16),
             pltpu.VMEM((16, 2, 128, 256), F32),
@@ -370,7 +395,7 @@
             pltpu.VMEM((16, 16, 256), BF16),
             pltpu.VMEM((15, 16, 256), BF16),
             dma((12,)), dma, dma, dma((8,)), dma((8,)),
-            dma((4, 4)), dma((4, 4)), dma((4, 2)), dma((4, 2)), dma((4,)), dma((4,)),
+            dma((5, 4)), dma((5, 4)), dma((5, 2)), dma((5, 2)), dma((5,)), dma((5,)),
             dma((15,)), dma((15,)), dma((15,)), dma((15,)),
         ],
         compiler_params=pltpu.CompilerParams(

time: 57.3 us -> 53.2 us (0.928)
  Pallas kernels: 56.6 us -> 52.4 us
    pallas_call x1, Pallas kernels: 53.8 us -> 49.6 us  [shards(): pl.pallas_call(relay, out_shape=(shape((16, 16, 256), BF16), shape((256,...]
where the time goes in v5:
time: 53.2 us; the launch traced here: 53.1 us
  Pallas kernels  52.4 us (98%)
  between operations  0.64 us (1%)
    pallas_call x1, Pallas kernels, shards(): pl.pallas_call(relay, out_shape=(shape((16, 16, 256), BF16), shape((256,...  49.6 us
    pallas_call x1, Pallas kernels, shards(): pl.pallas_call(finish, out_shape=(shape((1, 256, 1024), F32), shape((1, 6...  2.82 us

profile of v5, /device:TPU:1, one launch (start us, length us, event | category | flops | bytes accessed | tf_op | source)
XLA Modules:
  0.0 53.1 jit_solution(12042303226762359655)
XLA Ops:
  0.6 49.6 %shard_map.94 = (bf16[16,16,256]{2,1,0:T(8,128)(2,1)}, bf16[256,128]{1,0:T(8,128)(2,1)}, f32[256,128]{1,0:T(8,128)}) custom-call(bf16[4096,256]{1,0:T(8,128)(2,1)} %basis_hbm.3, f32[1,4096]{1,0:T(1,128)} %gain_hbm.1, bf16[1,4096,1024]{2,1,0:T(8,128)(2,1)} %value_hbm.3, bf16[1,1024,256]{2,1,0:T(8,128)(2,1)} %out_hbm.3, bf16[2,128,256]{2,1,0:T(8,128)(2,1)} %c_hbm.1, ...), custom_call_target="tpu_custom_call" | custom-call | tf_op jit(solution)/shard_map/pallas_call | solution.py:364
  50.2 2.8 %shard_map.95 = (f32[1,256,1024]{2,1,0:T(8,128)}, f32[1,64,256]{2,1,0:T(8,128)}, f32[1,256]{1,0:T(1,128)}) custom-call(bf16[16,16,256]{2,1,0:T(8,128)(2,1)} %get-tuple-element.6.factor_hbm, bf16[256,128]{1,0:T(8,128)(2,1)} %get-tuple-element.7.folded_hbm, f32[256,128]{1,0:T(8,128)} %get-tuple-element.8.own_gain_hbm, bf16[1,1024,256]{2,1,0:T(8,128)(2,1)} %out_hbm.3, ...), custom_call_target="tpu_custom_call" | custom-call | tf_op jit(solution)/shard_map/pallas_call | solution.py:405

commit v6 on v5

--- a/solution.py
+++ b/solution.py
@@ -9,7 +9,7 @@
 MESH = pl.DeviceIdType.MESH
 F32 = jnp.float32
 BF16 = jnp.bfloat16
-VMEM_LIMIT = 58 * 1024 * 1024
+VMEM_LIMIT = 44 * 1024 * 1024
 
 
 def mm(a, b, dims=((1,), (0,))):
@@ -84,8 +84,8 @@
 
 def relay(
     basis_hbm, gain_hbm, value_hbm, out_hbm, c_hbm, cot_hbm, seg_hbm,
-    whole, folded_ref, own_gain_ref,
-    out, value, value_cols, basis_half, basis, gain_half, gain, c_ref, cot_ref, seg_ref,
+    whole, out, basis_own, value_own, folded_ref, own_gain_ref,
+    value, value_cols, basis_half, basis, gain_half, gain, c_ref, cot_ref, seg_ref,
     part_n, part_nb, slot_n, gain_pad, every, xs, ps, es, hs, invs, part, part_b, slots,
     load_sem, n_send, n_recv, z_send, z_recv, y_send, y_recv, x_send, x_recv, c_send, c_recv,
     rs_send, rs_recv, ag_send, ag_recv,
@@ -93,7 +93,7 @@
     at = Place()
     width = basis.shape[0]
     half = width // 2
-    cuts = (0, 512, 1024, 2048)
+    cuts = (0, 512, 1024, 1536, 2048)
     start = pl.multiple_of(at.core * half, half)
 
     def load(i, src, dst):
@@ -106,7 +106,7 @@
         load(1, basis_hbm.at[pl.ds(start, half), :], basis_half),
         load(2, out_hbm.at[0], out),
     ]
-    for i in range(3):
+    for i in range(len(cuts) - 1):
         size = cuts[i + 1] - cuts[i]
         rows = pl.ds(pl.multiple_of(start + cuts[i], 512), size)
         early.append(load(3 + i, value_hbm.at[0, rows, :], value.at[pl.ds(cuts[i], size), :]))
@@ -115,25 +115,32 @@
     peers += [at.x_peer(1), at.x_peer(3)]
     for peer in peers:
         pl.semaphore_signal(barrier, inc=1, device_id=peer, device_id_type=MESH)
+    own_rows = pl.ds(pl.multiple_of(at.d * 256, 256), 256)
     cols = pl.ds(pl.multiple_of((at.d // 2) * 128, 128), 128)
     late = [
-        load(6, basis_hbm, basis),
-        load(7, value_hbm.at[0, :, cols], value_cols),
-        load(8, gain_hbm, gain),
-        load(9, c_hbm, c_ref),
-        load(10, seg_hbm, seg_ref),
-        load(11, cot_hbm, cot_ref),
+        load(7, basis_hbm, basis),
+        load(8, value_hbm.at[0, :, cols], value_cols),
+        load(9, gain_hbm, gain),
+        load(10, c_hbm, c_ref),
+        load(11, seg_hbm, seg_ref),
+        load(12, cot_hbm, cot_ref),
+        load(13, basis_hbm.at[own_rows, :], basis_own),
+        load(14, value_hbm.at[0, own_rows, :], value_own),
     ]
 
     partial = jnp.zeros((256, 256), F32)
     for copy in early[:3]:
         copy.wait()
-    for i in range(3):
+    before = None
+    for i in range(len(cuts) - 1):
         lanes = slice(cuts[i], cuts[i + 1])
         scaled = (basis_half[lanes, :].astype(F32).T * gain_half[0:1, lanes]).astype(BF16)
         early[3 + i].wait()
         through = mm(value[lanes, :], out[...]).astype(BF16)
-        partial = partial + mm(scaled, through)
+        if before is not None:
+            partial = partial + mm(*before)
+        before = (scaled, through)
+    partial = partial + mm(*before)
     part_n[...] = partial.reshape(8, 32, 256)
     part_nb[...] = partial.astype(BF16).reshape(8, 32, 256)
 
@@ -170,7 +177,7 @@
     cs = [c_ref[m].astype(F32) for m in range(micros)]
     hh = [mm(c_ref[m], gram_b) for m in range(micros)]
 
-    bounds = (0, 1, 2, 4, 6, 8)
+    bounds = (0, 1, 2, 4, 6, 7, 8)
     over_y, over_x, across = [], [], []
 
     def arrived(z):
@@ -258,6 +265,7 @@
     start_y(4)
     start_core(0)
     start_x(2)
+    start_y(5)
     start_core(1)
     start_x(3)
     across[0].wait_recv()
@@ -267,16 +275,23 @@
         ng = forward(s, ng)
     start_core(2)
     start_x(4)
+    start_x(5)
     start_core(3)
     across[2].wait_recv()
     for s in (3, 4, 5, 6):
         ng = forward(s, ng)
     start_core(4)
     across[3].wait_recv()
-    for s in (7, 8, 9, 10):
+    for s in (7, 8, 9):
+        ng = forward(s, ng)
+    start_core(5)
+    for s in (10,):
         ng = forward(s, ng)
     across[4].wait_recv()
-    for s in (11, 12, 13, 14, 15):
+    for s in (11, 12):
+        ng = forward(s, ng)
+    across[5].wait_recv()
+    for s in (13, 14, 15):
         ng = forward(s, ng)
 
     gs = [cot_ref[m].astype(F32) for m in range(micros)]
@@ -316,22 +331,9 @@
         copy.wait()
 
 
-def finish(factor_hbm, folded_hbm, own_gain_hbm, out_hbm, basis_hbm, value_hbm, gv_hbm, go_hbm, gg_hbm,
-           factor_ref, folded, own_gain, out, basis, value, gv, go, gg, load_sem, store_sem):
+def finish(factor_ref, out, basis, value, folded, own_gain, gv_hbm, go_hbm, gg_hbm,
+           gv, go, gg, store_sem):
     d = lax.axis_index("dp")
-    rows = pl.ds(pl.multiple_of(d * 256, 256), 256)
-    loads = [
-        pltpu.make_async_copy(factor_hbm, factor_ref, load_sem.at[0]),
-        pltpu.make_async_copy(basis_hbm.at[rows, :], basis, load_sem.at[1]),
-        pltpu.make_async_copy(out_hbm.at[0], out, load_sem.at[2]),
-        pltpu.make_async_copy(own_gain_hbm, own_gain, load_sem.at[3]),
-        pltpu.make_async_copy(value_hbm.at[0, rows, :], value, load_sem.at[4]),
-        pltpu.make_async_copy(folded_hbm, folded, load_sem.at[5]),
-    ]
-    for load in loads:
-        load.start()
-    for load in loads:
-        load.wait()
     factor = factor_ref[...].reshape(256, 256)
     left = mm(basis[...], factor).astype(BF16)
     gain = own_gain[:, :1]
@@ -361,17 +363,21 @@
     hbm = pl.BlockSpec(memory_space=pltpu.HBM)
     dma = pltpu.SemaphoreType.DMA
     shape = jax.ShapeDtypeStruct
+    operands = (basis_matrix, section_gains, value_weight, out_weight, coeffs, cotangent, segment_ids)
+    operands = [pltpu.with_memory_space_constraint(x, pltpu.HBM) for x in operands]
     handed = pl.pallas_call(
         relay,
         out_shape=(
             shape((16, 16, 256), BF16),
+            shape((1024, 256), BF16),
+            shape((256, 256), BF16),
+            shape((256, 1024), BF16),
             shape((256, 128), BF16),
             shape((256, 128), F32),
         ),
         in_specs=[hbm] * 7,
-        out_specs=(vmem,) * 3,
+        out_specs=(vmem,) * 6,
         scratch_shapes=[
-            pltpu.VMEM((1024, 256), BF16),
             pltpu.VMEM((2048, 1024), BF16),
             pltpu.VMEM((4096, 128), BF16),
             pltpu.VMEM((2048, 256), BF16),
@@ -394,14 +400,14 @@
             pltpu.VMEM((16, 16, 256), F32),
             pltpu.VMEM((16, 16, 256), BF16),
             pltpu.VMEM((15, 16, 256), BF16),
-            dma((12,)), dma, dma, dma((8,)), dma((8,)),
-            dma((5, 4)), dma((5, 4)), dma((5, 2)), dma((5, 2)), dma((5,)), dma((5,)),
+            dma((15,)), dma, dma, dma((8,)), dma((8,)),
+            dma((6, 4)), dma((6, 4)), dma((6, 2)), dma((6, 2)), dma((6,)), dma((6,)),
             dma((15,)), dma((15,)), dma((15,)), dma((15,)),
         ],
         compiler_params=pltpu.CompilerParams(
             collective_id=0, has_side_effects=True, vmem_limit_bytes=VMEM_LIMIT
         ),
-    )(basis_matrix, section_gains, value_weight, out_weight, coeffs, cotangent, segment_ids)
+    )(*operands)
     return pl.pallas_call(
         finish,
         out_shape=(
@@ -409,23 +415,16 @@
             shape((1, 64, 256), F32),
             shape((1, 256), F32),
         ),
-        in_specs=[hbm] * 6,
+        in_specs=[vmem] * 6,
         out_specs=(hbm,) * 3,
         scratch_shapes=[
-            pltpu.VMEM((16, 16, 256), BF16),
-            pltpu.VMEM((256, 128), BF16),
-            pltpu.VMEM((256, 128), F32),
-            pltpu.VMEM((1024, 256), BF16),
-            pltpu.VMEM((256, 256), BF16),
-            pltpu.VMEM((256, 1024), BF16),
             pltpu.VMEM((256, 1024), F32),
             pltpu.VMEM((128, 256), F32),
             pltpu.VMEM((1, 256), F32),
             dma((6,)),
-            dma((6,)),
         ],
-        compiler_params=pltpu.CompilerParams(vmem_limit_bytes=VMEM_LIMIT),
-    )(*handed, out_weight, basis_matrix, value_weight)
+        compiler_params=pltpu.CompilerParams(vmem_limit_bytes=16 * 1024 * 1024),
+    )(*handed)
 
 
 def solution(mesh):

time: 53.2 us -> 51.5 us (0.968)
  Pallas kernels: 52.4 us -> 50.7 us
    pallas_call x1, Pallas kernels: 2.82 us -> 1.39 us  [shards(): pl.pallas_call(finish, out_shape=(shape((1, 256, 1024), F32), shape((1, 6...]
where the time goes in v6:
time: 51.5 us; the launch traced here: 51.4 us
  Pallas kernels  50.7 us (98%)
  between operations  0.64 us (1%)
    pallas_call x1, Pallas kernels, shards(): pl.pallas_call(relay, out_shape=(shape((16, 16, 256), BF16), shape((1024,...  49.3 us
    pallas_call x1, Pallas kernels, shards(): pl.pallas_call(finish, out_shape=(shape((1, 256, 1024), F32), shape((1, 6...  1.39 us

profile of v6, /device:TPU:1, one launch (start us, length us, event | category | flops | bytes accessed | tf_op | source)
XLA Modules:
  0.0 51.4 jit_solution(10262142032188204934)
XLA Ops:
  0.6 49.3 %shard_map.94 = (bf16[16,16,256]{2,1,0:T(8,128)(2,1)S(1)}, bf16[1024,256]{1,0:T(8,128)(2,1)S(1)}, bf16[256,256]{1,0:T(8,128)(2,1)S(1)}, bf16[256,1024]{1,0:T(8,1...) custom-call(bf16[4096,256]{1,0:T(8,128)(2,1)} %basis_hbm.1, f32[1,4096]{1,0:T(1,128)} %gain_hbm.1, ...), custom_call_target="tpu_custom_call" | custom-call | tf_op jit(solution)/shard_map/pallas_call | solution.py:368
  50.0 1.4 %shard_map.95 = (f32[1,256,1024]{2,1,0:T(8,128)}, f32[1,64,256]{2,1,0:T(8,128)}, f32[1,256]{1,0:T(1,128)}) custom-call(bf16[16,16,256]{2,1,0:T(8,128)(2,1)S(1)} %get-tuple-element.9.factor_ref, bf16[1024,256]{1,0:T(8,128)(2,1)S(1)} %get-tuple-element.10.out, bf16[256,256]{1,0:T(8,128)(2,1)S(1)} %get-tuple-element.11.basis, ...), custom_call_target="tpu_custom_call" | custom-call | tf_op jit(solution)/shard_map/pallas_call | solution.py:411

commit v7 on v6

--- a/solution.py
+++ b/solution.py
@@ -34,66 +34,59 @@
     def __init__(self):
         self.s = lax.axis_index("section")
         self.d = lax.axis_index("dp")
-        self.z = self.s // 2
-        self.xl = self.s % 2
-        self.y = self.d // 4
-        self.xh = (self.d // 2) % 2
-        self.core = self.d % 2
-        self.x = self.xh * 2 + self.xl
-
-    def dp_peer(self, k):
-        return (self.s, (self.d + k) % 16)
+        self.z = lax.div(self.s, 2)
+        self.xl = lax.rem(self.s, 2)
+        self.y = lax.div(self.d, 4)
+        self.xh = lax.rem(lax.div(self.d, 2), 2)
+        self.core = lax.rem(self.d, 2)
+        x = self.xh * 2 + self.xl
+        self.ys = [lax.rem(self.y + k, 4) for k in range(4)]
+        self.xhs = [self.xh] + [lax.div(lax.rem(x + k, 4), 2) for k in range(1, 4)]
+        self.twin = self.s + 1 - 2 * self.xl
+        self.rows = [y * 4 for y in self.ys]
 
     def z_peer(self, k):
-        return (((self.z + k) % 8) * 2 + self.xl, self.d)
+        return (lax.rem(self.z + k, 8) * 2 + self.xl, self.d)
+
+    def member(self, dx, dy, core):
+        section = self.s if dx % 2 == 0 else self.twin
+        return (section, self.rows[dy] + self.xhs[dx] * 2 + core)
 
     def y_peer(self, k):
-        return (self.s, ((self.y + k) % 4) * 4 + self.xh * 2 + self.core)
+        return self.member(0, k, self.core)
 
     def x_peer(self, k):
-        x = (self.x + k) % 4
-        return (self.z * 2 + x % 2, self.y * 4 + (x // 2) * 2 + self.core)
+        return self.member(k, 0, self.core)
 
     def core_peer(self):
-        return (self.s, self.y * 4 + self.xh * 2 + (self.core + 1) % 2)
-
-
-def piece_of(d):
-    return (d % 2) * 8 + d // 2
-
-
-def send(src, dst, send_sem, recv_sem, peer):
-    copy = pltpu.make_async_remote_copy(
+        return self.member(0, 0, 1 - self.core)
+
+
+def remote(src, dst, send_sem, recv_sem, peer):
+    return pltpu.make_async_remote_copy(
         src_ref=src, dst_ref=dst, send_sem=send_sem, recv_sem=recv_sem,
         device_id=peer, device_id_type=MESH,
     )
+
+
+def send(src, dst, send_sem, recv_sem, peer):
+    copy = remote(src, dst, send_sem, recv_sem, peer)
     copy.start()
     return copy
-
-
-def far_first(at):
-    hops = lambda o: min(o[0], 4 - o[0]) + 2 * o[1]
-    offsets = [(y, xh, c) for y in range(4) for xh in range(2) for c in range(2) if (y, xh, c) != (0, 0, 0)]
-    offsets.sort(key=lambda o: -hops(o))
-    peers = []
-    for y, xh, c in offsets:
-        y_to, xh_to, c_to = (at.y + y) % 4, (at.xh + xh) % 2, (at.core + c) % 2
-        peers.append(((at.s, y_to * 4 + xh_to * 2 + c_to), c_to * 8 + y_to * 2 + xh_to))
-    return peers
 
 
 def relay(
     basis_hbm, gain_hbm, value_hbm, out_hbm, c_hbm, cot_hbm, seg_hbm,
     whole, out, basis_own, value_own, folded_ref, own_gain_ref,
     value, value_cols, basis_half, basis, gain_half, gain, c_ref, cot_ref, seg_ref,
-    part_n, part_nb, slot_n, gain_pad, every, xs, ps, es, hs, invs, part, part_b, slots,
+    part_n, part_nb, slot_n, gain_pad, every, xs, grads, es, hs, invs, left_t, part, part_b, slots, summed,
     load_sem, n_send, n_recv, z_send, z_recv, y_send, y_recv, x_send, x_recv, c_send, c_recv,
     rs_send, rs_recv, ag_send, ag_recv,
 ):
     at = Place()
     width = basis.shape[0]
     half = width // 2
-    cuts = (0, 512, 1024, 1536, 2048)
+    cuts = (0, 256, 768, 1280, 1792, 2048)
     start = pl.multiple_of(at.core * half, half)
 
     def load(i, src, dst):
@@ -101,51 +94,50 @@
         copy.start()
         return copy
 
-    early = [
-        load(0, gain_hbm.at[:, pl.ds(start, half)], gain_half),
-        load(1, basis_hbm.at[pl.ds(start, half), :], basis_half),
-        load(2, out_hbm.at[0], out),
-    ]
+    gain_half_load = load(0, gain_hbm.at[:, pl.ds(start, half)], gain_half)
+    early = []
     for i in range(len(cuts) - 1):
         size = cuts[i + 1] - cuts[i]
-        rows = pl.ds(pl.multiple_of(start + cuts[i], 512), size)
-        early.append(load(3 + i, value_hbm.at[0, rows, :], value.at[pl.ds(cuts[i], size), :]))
+        rows, here = pl.ds(pl.multiple_of(start + cuts[i], 256), size), pl.ds(cuts[i], size)
+        early.append((
+            load(1 + 2 * i, basis_hbm.at[rows, :], basis_half.at[here, :]),
+            load(2 + 2 * i, value_hbm.at[0, rows, :], value.at[here, :]),
+        ))
+    out_load = load(11, out_hbm.at[0], out)
     barrier = pltpu.get_barrier_semaphore()
-    peers = [at.z_peer(k) for k in (4, 3, 5, 2, 6, 1, 7)] + [at.dp_peer(k) for k in range(1, 16)]
-    peers += [at.x_peer(1), at.x_peer(3)]
+    peers = [at.z_peer(k) for k in (4, 3, 5, 2, 6, 1, 7)]
+    peers += [at.member(dx, dy, core) for dx in (1, 3) for dy in (2, 1, 3, 0) for core in (0, 1)]
+    peers += [at.member(0, dy, core) for dy in (2, 1, 3) for core in (0, 1)] + [at.core_peer()]
     for peer in peers:
         pl.semaphore_signal(barrier, inc=1, device_id=peer, device_id_type=MESH)
     own_rows = pl.ds(pl.multiple_of(at.d * 256, 256), 256)
-    cols = pl.ds(pl.multiple_of((at.d // 2) * 128, 128), 128)
+    cols = pl.ds(pl.multiple_of(lax.div(at.d, 2) * 128, 128), 128)
     late = [
-        load(7, basis_hbm, basis),
-        load(8, value_hbm.at[0, :, cols], value_cols),
-        load(9, gain_hbm, gain),
-        load(10, c_hbm, c_ref),
-        load(11, seg_hbm, seg_ref),
-        load(12, cot_hbm, cot_ref),
-        load(13, basis_hbm.at[own_rows, :], basis_own),
-        load(14, value_hbm.at[0, own_rows, :], value_own),
+        load(12, basis_hbm, basis),
+        load(13, value_hbm.at[0, :, cols], value_cols),
+        load(14, gain_hbm, gain),
+        load(15, c_hbm, c_ref),
+        load(16, seg_hbm, seg_ref),
+        load(17, cot_hbm, cot_ref),
+        load(18, basis_hbm.at[own_rows, :], basis_own),
+        load(19, value_hbm.at[0, own_rows, :], value_own),
     ]
 
-    partial = jnp.zeros((256, 256), F32)
-    for copy in early[:3]:
-        copy.wait()
-    before = None
+    gain_half_load.wait()
+    wide = jnp.zeros((256, out.shape[0]), F32)
     for i in range(len(cuts) - 1):
         lanes = slice(cuts[i], cuts[i + 1])
+        early[i][0].wait()
         scaled = (basis_half[lanes, :].astype(F32).T * gain_half[0:1, lanes]).astype(BF16)
-        early[3 + i].wait()
-        through = mm(value[lanes, :], out[...]).astype(BF16)
-        if before is not None:
-            partial = partial + mm(*before)
-        before = (scaled, through)
-    partial = partial + mm(*before)
+        early[i][1].wait()
+        wide = wide + mm(scaled, value[lanes, :])
+    out_load.wait()
+    partial = mm(wide.astype(BF16), out[...])
     part_n[...] = partial.reshape(8, 32, 256)
     part_nb[...] = partial.astype(BF16).reshape(8, 32, 256)
 
     pl.semaphore_wait(barrier, len(peers))
-    other = (at.core + 1) % 2
+    other = 1 - at.core
     swap = send(part_nb.at[other * 4 + at.y], slot_n, n_send, n_recv, at.core_peer())
     swap.wait_recv()
     own = every.at[at.core, at.z, at.xl, at.y]
@@ -177,17 +169,14 @@
     cs = [c_ref[m].astype(F32) for m in range(micros)]
     hh = [mm(c_ref[m], gram_b) for m in range(micros)]
 
-    bounds = (0, 1, 2, 4, 6, 7, 8)
+    bounds = (0, 2, 4, 6, 8)
     over_y, over_x, across = [], [], []
 
     def arrived(z):
         @pl.when(at.z != z)
         def _():
             there = every.at[at.core, z, at.xl, at.y]
-            pltpu.make_async_remote_copy(
-                src_ref=there, dst_ref=there, send_sem=z_send.at[0], recv_sem=z_recv.at[z],
-                device_id=at.core_peer(), device_id_type=MESH,
-            ).wait_recv()
+            remote(there, there, z_send.at[0], z_recv.at[z], at.core_peer()).wait_recv()
 
     def planes(q):
         return pl.ds(bounds[q], bounds[q + 1] - bounds[q])
@@ -261,74 +250,110 @@
     sent(over_y[1])
     start_y(3)
     start_x(1)
-    sent(over_y[2])
-    start_y(4)
     start_core(0)
     start_x(2)
-    start_y(5)
     start_core(1)
     start_x(3)
     across[0].wait_recv()
-    across[1].wait_recv()
     ng = onward(0)
     for s in (0, 1, 2):
         ng = forward(s, ng)
+    across[1].wait_recv()
     start_core(2)
-    start_x(4)
-    start_x(5)
+    for s in (3, 4, 5, 6):
+        ng = forward(s, ng)
     start_core(3)
     across[2].wait_recv()
-    for s in (3, 4, 5, 6):
+    for s in (7, 8, 9, 10):
         ng = forward(s, ng)
-    start_core(4)
     across[3].wait_recv()
-    for s in (7, 8, 9):
+    for s in (11, 12, 13, 14, 15):
         ng = forward(s, ng)
-    start_core(5)
-    for s in (10,):
-        ng = forward(s, ng)
-    across[4].wait_recv()
-    for s in (11, 12):
-        ng = forward(s, ng)
-    across[5].wait_recv()
-    for s in (13, 14, 15):
-        ng = forward(s, ng)
+
+    twin = at.twin
+    lanes_here = pl.ds(pl.multiple_of(at.xh * 128, 128), 128)
+    lanes_over = pl.ds(pl.multiple_of((1 - at.xh) * 128, 128), 128)
+
+    def left_factor(i, s, lanes):
+        for m in range(micros):
+            mixed = mm(mixings[m][0], xs[s, m, :, lanes])
+            left_t[i, :, m * 128 : (m + 1) * 128] = mixed.T.astype(BF16)
 
     gs = [cot_ref[m].astype(F32) for m in range(micros)]
+    both = range(micros)
     for s in reversed(range(16)):
+        for m in both:
+            grads[s, m] = gs[m].astype(BF16)
+        if s == 0:
+            break
         n = step_of(s)
-        both = range(micros)
         ps_ = [mm(mixings[m][1], gs[m].astype(BF16)) for m in both]
-        pb_ = [p.astype(BF16) for p in ps_]
-        qs_ = [mm(p, n, ((1,), (1,))) for p in pb_] if s > 0 else []
-        for m in both:
-            ps[s, m] = pb_[m]
-            if s > 0:
-                inv = invs[s, m][:, :1]
-                t = jnp.sum(ps_[m] * es[s, m], axis=1, keepdims=True)
-                gs[m] = (gs[m] - (inv * inv * inv * t * (1.0 / width)) * hs[s, m]) + inv * qs_[m]
-
-    rows = micros * xs.shape[2]
-    total = mm(xs[at.s].reshape(rows, 256), ps[at.s].reshape(rows, 256), ((0,), (0,)))
-    part[...] = total.reshape(16, 16, 256)
-    part_b[...] = total.astype(BF16).reshape(16, 16, 256)
-    others = far_first(at)
-    pieces = [
-        send(part_b.at[piece], slots.at[i], rs_send.at[i], rs_recv.at[i], peer)
-        for i, (peer, piece) in enumerate(others)
+        qs_ = [mm(p.astype(BF16), n, ((1,), (1,))) for p in ps_]
+        for m in both:
+            inv = invs[s, m][:, :1]
+            t = jnp.sum(ps_[m] * es[s, m], axis=1, keepdims=True)
+            gs[m] = (gs[m] - (inv * inv * inv * t * (1.0 / width)) * hs[s, m]) + inv * qs_[m]
+        if s == 15:
+            left_factor(0, twin, lanes_here)
+        if s == 14:
+            left_factor(1, at.s, lanes_over)
+
+    rows = micros * 128
+    over = mm(left_t[1], grads[at.s].reshape(rows, 256))
+    part_b[1] = over.astype(BF16).reshape(4, 32, 256)
+    pieces = []
+    for i, dy in enumerate((2, 1, 3, 0)):
+        j = 2 * i + at.core
+        pieces.append(send(
+            part_b.at[1, at.ys[dy]], slots.at[j], rs_send.at[i], rs_recv.at[j],
+            (at.twin, at.rows[dy] + (1 - at.xh) * 2 + 1)))
+    here = mm(left_t[0], grads[twin].reshape(rows, 256))
+    part[...] = here.reshape(4, 32, 256)
+    part_b[0] = here.astype(BF16).reshape(4, 32, 256)
+    for i, dy in enumerate((2, 1, 3)):
+        j = 8 + 2 * i + at.core
+        pieces.append(send(
+            part_b.at[0, at.ys[dy]], slots.at[j], rs_send.at[4 + i], rs_recv.at[j],
+            at.member(0, dy, 1)))
+    beside = remote(part_b.at[0, at.y], slots.at[14], rs_send.at[7], rs_recv.at[14], at.core_peer())
+    place = whole.at[at.xh, at.y]
+    spread = [
+        remote(summed, place, ag_send.at[i, j], ag_recv.at[i, j], at.member(dx, dy, at.core))
+        for i, dy in enumerate((2, 1, 3, 0)) for j, dx in enumerate((1, 3))
     ]
-    mine = part[piece_of(at.d)]
-    for i in reversed(range(15)):
-        pieces[i].wait_recv()
-        mine = mine + slots[i].astype(F32)
-    summed = whole.at[piece_of(at.d)]
-    summed[...] = mine.astype(BF16)
-    spread = [
-        send(summed, summed, ag_send.at[i], ag_recv.at[i], peer) for i, (peer, piece) in enumerate(others)
-    ]
-    sent([swap] + over_z + sum(over_y[3:], []) + sum(over_x, []) + across + pieces)
+    hand = remote(summed, summed, rs_send.at[8], rs_recv.at[15], at.core_peer())
+
+    @pl.when(at.core == 0)
+    def _():
+        beside.start()
+        hand.wait_recv()
+
+    @pl.when(at.core == 1)
+    def _():
+        mine = part[at.y]
+        for j in (14, 12, 13, 10, 11, 8, 9, 6, 7, 4, 5, 2, 3, 0, 1):
+            remote(slots.at[j], slots.at[j], rs_send.at[0], rs_recv.at[j], at.core_peer()).wait_recv()
+            mine = mine + slots[j].astype(F32)
+        summed[...] = mine.astype(BF16)
+        hand.start()
+
     for copy in spread:
-        copy.wait()
+        copy.start()
+    sent([swap] + over_z + sum(over_y[2:], []) + sum(over_x, []) + across + pieces)
+    sent(spread)
+
+    @pl.when(at.core == 0)
+    def _():
+        beside.wait_send()
+
+    @pl.when(at.core == 1)
+    def _():
+        hand.wait_send()
+
+    for i, dy in enumerate((2, 1, 3, 0)):
+        for j, dx in enumerate((1, 3)):
+            there = whole.at[at.xhs[4 - dx], at.ys[(4 - dy) % 4]]
+            remote(there, there, ag_send.at[0, 0], ag_recv.at[i, j], at.core_peer()).wait_recv()
 
 
 def finish(factor_ref, out, basis, value, folded, own_gain, gv_hbm, go_hbm, gg_hbm,
@@ -368,7 +393,7 @@
     handed = pl.pallas_call(
         relay,
         out_shape=(
-            shape((16, 16, 256), BF16),
+            shape((2, 4, 32, 256), BF16),
             shape((1024, 256), BF16),
             shape((256, 256), BF16),
             shape((256, 1024), BF16),
@@ -397,12 +422,14 @@
             pltpu.VMEM((16, 2, 128, 256), F32),
             pltpu.VMEM((16, 2, 128, 256), F32),
             pltpu.VMEM((16, 2, 128, 128), F32),
-            pltpu.VMEM((16, 16, 256), F32),
-            pltpu.VMEM((16, 16, 256), BF16),
-            pltpu.VMEM((15, 16, 256), BF16),
-            dma((15,)), dma, dma, dma((8,)), dma((8,)),
-            dma((6, 4)), dma((6, 4)), dma((6, 2)), dma((6, 2)), dma((6,)), dma((6,)),
-            dma((15,)), dma((15,)), dma((15,)), dma((15,)),
+            pltpu.VMEM((2, 128, 256), BF16),
+            pltpu.VMEM((4, 32, 256), F32),
+            pltpu.VMEM((2, 4, 32, 256), BF16),
+            pltpu.VMEM((15, 32, 256), BF16),
+            pltpu.VMEM((32, 256), BF16),
+            dma((20,)), dma, dma, dma((8,)), dma((8,)),
+            dma((4, 4)), dma((4, 4)), dma((4, 2)), dma((4, 2)), dma((4,)), dma((4,)),
+            dma((9,)), dma((16,)), dma((4, 2)), dma((4, 2)),
         ],
         compiler_params=pltpu.CompilerParams(
             collective_id=0, has_side_effects=True, vmem_limit_bytes=VMEM_LIMIT

time: 51.5 us -> 50 us (0.971)
  Pallas kernels: 50.7 us -> 49.3 us
    pallas_call x1, Pallas kernels: 49.3 us -> 47.9 us  [shards(): pl.pallas_call(relay, out_shape=(shape((2, 4, 32, 256), BF16), shape((102...]
where the time goes in v7:
time: 50 us; the launch traced here: 49.9 us
  Pallas kernels  49.3 us (99%)
  between operations  0.64 us (1%)
    pallas_call x1, Pallas kernels, shards(): pl.pallas_call(relay, out_shape=(shape((2, 4, 32, 256), BF16), shape((102...  47.9 us
    pallas_call x1, Pallas kernels, shards(): pl.pallas_call(finish, out_shape=(shape((1, 256, 1024), F32), shape((1, 6...  1.39 us

profile of v7, /device:TPU:1, one launch (start us, length us, event | category | flops | bytes accessed | tf_op | source)
XLA Modules:
  0.0 49.9 jit_solution(17217308107617214789)
XLA Ops:
  0.6 47.9 %shard_map.94 = (bf16[2,4,32,256]{3,2,1,0:T(8,128)(2,1)S(1)}, bf16[1024,256]{1,0:T(8,128)(2,1)S(1)}, bf16[256,256]{1,0:T(8,128)(2,1)S(1)}, bf16[256,1024]{1,0:T(...) custom-call(bf16[4096,256]{1,0:T(8,128)(2,1)} %basis_hbm.1, f32[1,4096]{1,0:T(1,128)} %gain_hbm.1, ...), custom_call_target="tpu_custom_call" | custom-call | tf_op jit(solution)/shard_map/pallas_call | solution.py:393
  48.5 1.4 %shard_map.95 = (f32[1,256,1024]{2,1,0:T(8,128)}, f32[1,64,256]{2,1,0:T(8,128)}, f32[1,256]{1,0:T(1,128)}) custom-call(bf16[2,4,32,256]{3,2,1,0:T(8,128)(2,1)S(1)} %get-tuple-element.9.factor_ref, bf16[1024,256]{1,0:T(8,128)(2,1)S(1)} %get-tuple-element.10.out, bf16[256,256]{1,0:T(8,128)(2,1)S(1)} %get-tuple-element.11.basis, ...), custom_call_target="tpu_custom_call" | custom-call | tf_op jit(solution)/shard_map/pallas_call | solution.py:438

commit v8 on v7

--- a/solution.py
+++ b/solution.py
@@ -112,16 +112,6 @@
         pl.semaphore_signal(barrier, inc=1, device_id=peer, device_id_type=MESH)
     own_rows = pl.ds(pl.multiple_of(at.d * 256, 256), 256)
     cols = pl.ds(pl.multiple_of(lax.div(at.d, 2) * 128, 128), 128)
-    late = [
-        load(12, basis_hbm, basis),
-        load(13, value_hbm.at[0, :, cols], value_cols),
-        load(14, gain_hbm, gain),
-        load(15, c_hbm, c_ref),
-        load(16, seg_hbm, seg_ref),
-        load(17, cot_hbm, cot_ref),
-        load(18, basis_hbm.at[own_rows, :], basis_own),
-        load(19, value_hbm.at[0, own_rows, :], value_own),
-    ]
 
     gain_half_load.wait()
     wide = jnp.zeros((256, out.shape[0]), F32)
@@ -130,6 +120,17 @@
         early[i][0].wait()
         scaled = (basis_half[lanes, :].astype(F32).T * gain_half[0:1, lanes]).astype(BF16)
         early[i][1].wait()
+        if i == len(cuts) - 2:
+            late = [
+                load(12, basis_hbm, basis),
+                load(13, value_hbm.at[0, :, cols], value_cols),
+                load(14, gain_hbm, gain),
+                load(15, c_hbm, c_ref),
+                load(16, seg_hbm, seg_ref),
+                load(17, cot_hbm, cot_ref),
+                load(18, basis_hbm.at[own_rows, :], basis_own),
+                load(19, value_hbm.at[0, own_rows, :], value_own),
+            ]
         wide = wide + mm(scaled, value[lanes, :])
     out_load.wait()
     partial = mm(wide.astype(BF16), out[...])

time: 50 us -> 50 us (level)
  no operation moved by 1% of the time
where the time goes in v8:
time: 50 us; the launch traced here: 49.9 us
  Pallas kernels  49.3 us (99%)
  between operations  0.64 us (1%)
    pallas_call x1, Pallas kernels, shards(): pl.pallas_call(relay, out_shape=(shape((2, 4, 32, 256), BF16), shape((102...  47.9 us
    pallas_call x1, Pallas kernels, shards(): pl.pallas_call(finish, out_shape=(shape((1, 256, 1024), F32), shape((1, 6...  1.39 us

profile of v8, /device:TPU:1, one launch (start us, length us, event | category | flops | bytes accessed | tf_op | source)
XLA Modules:
  0.0 49.9 jit_solution(6510613998991984509)
XLA Ops:
  0.6 47.9 %shard_map.94 = (bf16[2,4,32,256]{3,2,1,0:T(8,128)(2,1)S(1)}, bf16[1024,256]{1,0:T(8,128)(2,1)S(1)}, bf16[256,256]{1,0:T(8,128)(2,1)S(1)}, bf16[256,1024]{1,0:T(...) custom-call(bf16[4096,256]{1,0:T(8,128)(2,1)} %basis_hbm.1, f32[1,4096]{1,0:T(1,128)} %gain_hbm.1, ...), custom_call_target="tpu_custom_call" | custom-call | tf_op jit(solution)/shard_map/pallas_call | solution.py:394
  48.5 1.4 %shard_map.95 = (f32[1,256,1024]{2,1,0:T(8,128)}, f32[1,64,256]{2,1,0:T(8,128)}, f32[1,256]{1,0:T(1,128)}) custom-call(bf16[2,4,32,256]{3,2,1,0:T(8,128)(2,1)S(1)} %get-tuple-element.9.factor_ref, bf16[1024,256]{1,0:T(8,128)(2,1)S(1)} %get-tuple-element.10.out, bf16[256,256]{1,0:T(8,128)(2,1)S(1)} %get-tuple-element.11.basis, ...), custom_call_target="tpu_custom_call" | custom-call | tf_op jit(solution)/shard_map/pallas_call | solution.py:439
